TPU v7x, 256 devices: a whole 4x4x8 slice. The times are simulated.
256 devices in a mesh: seq: 32 (over x, y, core), dp: 8 (over z).
Axes of the slice: x: 4, y: 4, z: 8, core: 2. Of those that a mesh axis runs over, the one named last changes fastest.
Arguments:
- frame_counts: int32 [8, 16], P('dp'), may hold values from 1 to 3072, 6144 in all within a row
- glu_out: bfloat16 [8, 6144, 1536], P('dp', 'seq'), may hold values from -40 to 40
- tap_weight: float32 [32, 1536], replicated, may hold values from -1 to 1
- bn_gain: float32 [1536], replicated, may hold values from 0.1 to 1.9
- bn_shift: float32 [1536], replicated, may hold values from -3 to 3
- proj_weight: bfloat16 [1536, 1536], replicated, may hold values from -0.15625 to 0.15625
- out_grad: bfloat16 [8, 6144, 1536], P('dp', 'seq'), may hold values from -6 to 6
Outputs:
- block_out: bfloat16 [8, 6144, 1536], P('dp', 'seq')
- frame_grad: bfloat16 [8, 6144, 1536], P('dp', 'seq')
- tap_grad: float32 [32, 1536], replicated
- gain_grad: float32 [1536], replicated
- shift_grad: float32 [1536], replicated
- proj_grad: float32 [1536, 1536], P(('seq', 'dp'))
Inputs may be any that keep to these rules, and one draw needn't show every extreme that they name: `frame_counts`: each row sums to 6144; the utterances lie one after another along the group's frames.
All inputs are finite; a program needn't handle non-finite values.
Results may differ from a plain program's by a relative error of at most 0.0049.
Values may be sent and summed in bfloat16 or wider, within the bound.
No kernel may reach another device: no remote copies, remote signals or barrier semaphores. Data moves between devices by JAX's collectives and lax.ppermute only.
A program may use at most 128 MiB of HBM per device.

v0:
```python
import functools

import jax
import jax.numpy as jnp
from jax import lax
from jax.experimental import pallas as pl
from jax.experimental.pallas import tpu as pltpu
from jax.sharding import Mesh, PartitionSpec as P

HALF = 16
KERNEL = 2 * HALF
EPSILON = 1e-05
SEQ = ("x", "y", "c")
PLANE = ("x", "y")
COLUMN = ("c", "z")
LANES = 128
TILE = 512
SUB = 8
BLOCKS = 4
GROUP = 4
F32 = jnp.float32


def shifted(value, axes, step):
    count = lax.axis_size(axes)
    pairs = [(i, i + step) for i in range(count) if 0 <= i + step < count]
    return lax.ppermute(value, axes, pairs)


def rotated(value, axis, step):
    count = lax.axis_size(axis)
    return lax.ppermute(value, axis, [(i, (i + step) % count) for i in range(count)])


def crossed(value, axis, bit):
    count = lax.axis_size(axis)
    return lax.ppermute(value, axis, [(i, i ^ bit) for i in range(count)])


def doubled(value, axis, bit):
    other = crossed(value, axis, bit)
    upper = (lax.axis_index(axis) & bit) != 0
    first, second = jnp.where(upper, other, value), jnp.where(upper, value, other)
    return jnp.concatenate([first, second])


def exchanged(blocks, axes):
    return lax.all_to_all(blocks, axes, 0, 0, tiled=True)


def gathered(value, axes):
    count = lax.axis_size(axes)
    return exchanged(jnp.broadcast_to(value[None], (count,) + value.shape), axes)


def merged(stats, count):
    means, squares = stats[:, 0], stats[:, 1]
    mean = jnp.mean(means, axis=0)
    spread = jnp.sum(jnp.square(means - mean), axis=0)
    return jnp.stack([mean, jnp.sum(squares, axis=0) + count * spread])


def segment_ids(counts, positions, frames):
    ends = jnp.cumsum(counts)
    found = jnp.sum((positions[:, None] >= ends[None, :]).astype(jnp.int32), axis=1)
    return jnp.where((positions >= 0) & (positions < frames), found, -1)


def window_mask(counts, first, frames, limit):
    row = lax.broadcasted_iota(jnp.int32, (KERNEL, frames + 4 * HALF), 1)
    owner = row + HALF - lax.broadcasted_iota(jnp.int32, row.shape, 0)
    ends = jnp.cumsum(counts)[:, None, None]
    same = jnp.all((first + row >= ends) == (first + owner >= ends), axis=0)
    inside = (owner >= 2 * HALF) & (owner < 2 * HALF + frames)
    valid = (first + row >= 0) & (first + row < limit)
    return (same & inside & valid).astype(jnp.bfloat16)


def shift_copies(source, copies):
    rows = copies.shape[1]
    for b in range(SUB):
        copies[b] = source[b : b + rows]


def lane_groups():
    tiles = [pl.ds(t * LANES, LANES) for t in range(TILE // LANES)]
    return [tiles[t : t + GROUP] for t in range(0, len(tiles), GROUP)]


def convolve(ids_ref, ids, copies, taps_ref, out_ref, rows, centre, tap_of, id_shift):
    offsets = [o for o in range(KERNEL + 1) if 0 <= tap_of(o) < KERNEL]
    for tiles in lane_groups():
        def step(j, carry, tiles=tiles):
            base = pl.multiple_of(j * SUB * BLOCKS, SUB * BLOCKS)
            own = [ids_ref[pl.ds(base + i * SUB + centre, SUB), :] for i in range(BLOCKS)]
            totals = [[jnp.zeros((SUB, LANES), F32) for _ in tiles] for _ in range(BLOCKS)]
            for low in range(SUB):
                steps = [o // SUB for o in offsets if o % SUB == low]
                reads = range(min(steps), max(steps) + BLOCKS)
                near = {i: ids[low, pl.ds(base + i * SUB + id_shift, SUB), :] for i in reads}
                keep = {(a, i): near[a + i] == own[i] for a in steps for i in range(BLOCKS)}
                for t, lanes in enumerate(tiles):
                    value = {i: copies[low, pl.ds(base + i * SUB, SUB), lanes] for i in reads}
                    for a in steps:
                        tap = taps_ref[pl.ds(tap_of(a * SUB + low), 1), lanes]
                        for i in range(BLOCKS):
                            term = jnp.where(keep[a, i], value[a + i], 0.0)
                            totals[i][t] = totals[i][t] + tap * term
            for i in range(BLOCKS):
                for t, lanes in enumerate(tiles):
                    out_ref[pl.ds(base + i * SUB, SUB), lanes] = totals[i][t]
            return carry

        lax.fori_loop(0, rows // (SUB * BLOCKS), step, 0)


def correlate(grad_ref, ids_ref, ids, copies, rows, first, out_ref):
    steps = range(KERNEL // SUB)
    for tiles in lane_groups():
        for low in range(SUB):
            def step(j, sums, tiles=tiles, low=low):
                base = pl.multiple_of(j * SUB * BLOCKS, SUB * BLOCKS)
                reads = range(len(steps) + BLOCKS - 1)
                own = [ids_ref[pl.ds(base + i * SUB + first + HALF, SUB), :] for i in range(BLOCKS)]
                near = [ids[low, pl.ds(base + i * SUB + first, SUB), :] for i in reads]
                keep = {(a, i): near[a + i] == own[i] for a in steps for i in range(BLOCKS)}
                out = list(sums)
                for t, lanes in enumerate(tiles):
                    value = [copies[low, pl.ds(base + i * SUB + first, SUB), lanes] for i in reads]
                    grads = [grad_ref[pl.ds(base + i * SUB, SUB), lanes] for i in range(BLOCKS)]
                    for a in steps:
                        at = t * len(steps) + a
                        for i in range(BLOCKS):
                            out[at] = out[at] + jnp.where(keep[a, i], value[a + i], 0.0) * grads[i]
                return tuple(out)

            start = tuple(jnp.zeros((SUB, LANES), F32) for _ in range(len(steps) * len(tiles)))
            sums = lax.fori_loop(0, rows // (SUB * BLOCKS), step, start)
            for t, lanes in enumerate(tiles):
                for a in steps:
                    total = jnp.sum(sums[t * len(steps) + a], axis=0, keepdims=True)
                    out_ref[pl.ds(a * SUB + low, 1), lanes] = total


def prepare(low_ref, mid_ref, high_ref, ids_ref, copies, ids):
    @pl.when(pl.program_id(0) == 0)
    def _():
        shift_copies(ids_ref[...], ids)

    parts = [low_ref[...][: 2 * HALF], mid_ref[...], high_ref[...][: 2 * HALF]]
    shift_copies(jnp.concatenate([p.astype(F32) for p in parts]), copies)


def conv_kernel(low_ref, mid_ref, high_ref, ids_ref, taps_ref, conv_ref, stats_ref, sent_ref, copies, ids):
    rows = conv_ref.shape[0]
    prepare(low_ref, mid_ref, high_ref, ids_ref, copies, ids)
    convolve(ids_ref, ids, copies, taps_ref, conv_ref, rows, HALF, lambda o: o, 0)
    inner = conv_ref[HALF : rows - HALF, :]
    mean = jnp.sum(inner, axis=0, keepdims=True) / inner.shape[0]
    stats = jnp.concatenate([mean, jnp.sum(jnp.square(inner - mean), axis=0, keepdims=True)])
    stats_ref[...] = stats
    sent_ref[...] = jnp.broadcast_to(stats[None], sent_ref.shape)


def moments_kernel(
    low_ref, mid_ref, high_ref, ids_ref, conv_ref, stats_ref, out_ref, copies, ids, centred
):
    rows = conv_ref.shape[0] - 2 * HALF
    prepare(low_ref, mid_ref, high_ref, ids_ref, copies, ids)
    centred[...] = conv_ref[HALF : HALF + rows, :] - stats_ref[0:1, :]
    correlate(centred, ids_ref, ids, copies, rows, HALF, out_ref)


def act_kernel(
    count, core_ref, low_ref, mid_ref, high_ref, ids_ref, conv_ref, back_ref, all_ref, own_ref, affine_ref,
    plain_ref, product_ref, swished_ref, grad_ref, kept_ref, given_ref, norm_ref, copies, ids, centred, taps,
):
    rows = conv_ref.shape[0] - 2 * HALF
    prepare(low_ref, mid_ref, high_ref, ids_ref, copies, ids)
    merge = all_ref.shape[0]
    means = [all_ref[i, 0:1, :] for i in range(merge)]
    mean = sum(means) / merge
    spread = sum(jnp.square(m - mean) for m in means)
    var = (sum(all_ref[i, 1:2, :] for i in range(merge)) + count * spread) / (count * merge)
    inverse = lax.rsqrt(var + EPSILON)
    norm_ref[...] = jnp.concatenate([mean, inverse])
    normed = (conv_ref[...] - mean) * inverse
    act = affine_ref[0:1, :] * normed + affine_ref[1:2, :]
    gate = jax.nn.sigmoid(act)
    grad = back_ref[...] * gate * (1.0 + act * (1.0 - gate))
    grad_ref[...] = grad
    swished_ref[...] = (act * gate)[HALF : HALF + rows].astype(jnp.bfloat16)
    inner, inner_normed = grad[HALF : HALF + rows], normed[HALF : HALF + rows]
    sums = [jnp.sum(inner, axis=0, keepdims=True), jnp.sum(inner * inner_normed, axis=0, keepdims=True)]
    centred[...] = inner
    correlate(centred, ids_ref, ids, copies, rows, HALF, taps)
    plain = plain_ref[...]
    product = inverse * (product_ref[...] + (own_ref[0:1, :] - mean) * plain)
    chips = kept_ref.shape[0]
    first = core_ref[0] == 0
    for i in range(chips):
        low, high = (
            jnp.concatenate([v[at : at + 1] for v in (taps, plain, product)] + [sums[at // chips]])
            for at in (i, chips + i)
        )
        kept_ref[i] = jnp.where(first, low, high)
        given_ref[i] = jnp.where(first, high, low)


def weight_kernel(_, own_ref, other_ref, own_grad_ref, other_grad_ref, left_ref, right_ref):
    over = (((0,), (0,)), ((), ()))
    part = lax.dot_general(own_ref[...], own_grad_ref[...], over, preferred_element_type=F32)
    part = part + lax.dot_general(other_ref[...], other_grad_ref[...], over, preferred_element_type=F32)
    part = part.astype(jnp.bfloat16)
    each, left = left_ref.shape[1:]
    for i in range(left_ref.shape[0]):
        left_ref[i] = part[i * each : (i + 1) * each, :left]
        right_ref[i, 0:each, :] = part[i * each : (i + 1) * each, left:]


def tap_kernel(total_rows, parts_ref, sums_ref, norm_ref, affine_ref, _, out_ref):
    scale = affine_ref[0:1, :] * norm_ref[1:2, :]
    shift, slope = sums_ref[0:1, :] / total_rows, sums_ref[1:2, :] / total_rows
    rest = scale * (parts_ref[0:1, :] - shift * parts_ref[1:2, :] - slope * parts_ref[2:3, :])
    height, size = out_ref.shape[1:]
    rows = []
    for _ in range(2):
        term = rest.astype(jnp.bfloat16).astype(F32)
        rows += [term[:, at : at + size] for at in range(0, rest.shape[1], size)]
        rest = rest - term
    rows.append(jnp.zeros((height - len(rows), size), F32))
    rows = jnp.concatenate(rows).astype(jnp.bfloat16)
    for i in range(out_ref.shape[0]):
        out_ref[i] = rows


def collect_kernel(left_ref, right_ref, out_ref, taps_ref):
    each = out_ref.shape[1]
    rows, left = left_ref.shape[1:]
    size = right_ref.shape[2]
    for all_ref, columns in ((left_ref, slice(0, left)), (right_ref, slice(left, left + size))):
        total = sum(all_ref[i, 0:rows, :].astype(F32) for i in range(all_ref.shape[0]))
        for i in range(out_ref.shape[0]):
            out_ref[i, :, columns] = total[i * each : (i + 1) * each]
    pieces = taps_ref.shape[1] // size
    for i in range(right_ref.shape[0]):
        terms = right_ref[i, rows:, :].astype(F32)
        terms = terms[:pieces] + terms[pieces : 2 * pieces]
        for piece in range(pieces):
            taps_ref[i : i + 1, piece * size : (piece + 1) * size] = terms[piece : piece + 1]


def frame_kernel(
    total_rows, ids_ref, conv_ref, grad_ref, norm_ref, sums_ref, affine_ref, taps_ref, out_ref, copies, ids, result
):
    rows = out_ref.shape[0]

    @pl.when(pl.program_id(0) == 0)
    def _():
        shift_copies(ids_ref[...], ids)

    mean, inverse = norm_ref[0:1, :], norm_ref[1:2, :]
    scale = affine_ref[0:1, :] * inverse
    shift, slope = sums_ref[0:1, :] / total_rows, sums_ref[1:2, :] / total_rows
    normed = (conv_ref[...] - mean) * inverse
    grad = scale * (grad_ref[...] - shift - normed * slope)
    for b in range(SUB):
        count = rows + 2 * HALF - (SUB if b else 0)
        copies[b, 0:count, :] = grad[b : b + count]

    convolve(
        ids_ref, ids, copies, taps_ref, result, rows, 2 * HALF, lambda o: KERNEL - o, HALF
    )
    out_ref[...] = result[...].astype(jnp.bfloat16)


PARAMS = pltpu.CompilerParams(vmem_limit_bytes=16 * 1024 * 1024)


def cut(shape, width):
    lead = (0,) * (len(shape) - 1)
    if shape == (1,):
        return pl.BlockSpec(memory_space=pltpu.SMEM)
    if shape[-1] != width:
        return pl.BlockSpec(shape, lambda i: lead + (0,))
    return pl.BlockSpec(shape[:-1] + (TILE,), lambda i: lead + (i,))


def call(kernel, width, ins, outs, scratch, weight=1):
    return pl.pallas_call(
        kernel,
        grid=(width // TILE,),
        in_specs=[cut(a.shape, width) for a in ins],
        out_specs=[cut(shape, width) for shape, _ in outs],
        out_shape=[jax.ShapeDtypeStruct(shape, kind) for shape, kind in outs],
        scratch_shapes=scratch,
        compiler_params=PARAMS,
        cost_estimate=pl.CostEstimate(
            flops=weight * 192 * KERNEL * width * 4, bytes_accessed=4 * 224 * width * 4, transcendentals=0
        ),
    )(*ins)


def local(frame_counts, glu_out, tap_weight, bn_gain, bn_shift, proj_weight, out_grad):
    inputs = glu_out[0]
    grads_in = out_grad[0]
    frames, width = inputs.shape
    half_width = width // 2
    devices = lax.axis_size(SEQ)
    chips, column = lax.axis_size(PLANE), lax.axis_size(COLUMN)
    total_rows = frames * chips * column
    core = lax.axis_index("c")
    rows = frames + 2 * HALF
    reach = frames + 4 * HALF - SUB
    bf16 = jnp.bfloat16

    up = jnp.concatenate([inputs[-2 * HALF :], grads_in[-HALF:]])
    down = jnp.concatenate([inputs[: 2 * HALF], grads_in[:HALF]])
    low, high = shifted(up, SEQ, 1), shifted(down, SEQ, -1)
    grads_wide = jnp.concatenate([low[2 * HALF :], grads_in, high[2 * HALF :]])

    first = lax.axis_index(SEQ) * frames - 2 * HALF
    positions = first + jnp.arange(frames + 4 * HALF, dtype=jnp.int32)
    segments = segment_ids(frame_counts[0], positions, frames * devices)
    segments = jnp.broadcast_to(segments[:, None], (frames + 4 * HALF, LANES))
    value_copies = pltpu.VMEM((SUB, reach, TILE), F32)
    id_copies = pltpu.VMEM((SUB, reach, LANES), jnp.int32)
    column_rows = pltpu.VMEM((frames, TILE), F32)

    conv, own_stats, sent = call(
        conv_kernel, width, [low, inputs, high, segments, tap_weight],
        [((rows, width), F32), ((2, width), F32), ((chips, 2, width), F32)],
        [value_copies, id_copies],
    )
    back = lax.dot_general(
        grads_wide, proj_weight, (((1,), (1,)), ((), ())), preferred_element_type=F32
    )
    own_stats, bn_gain, bn_shift = lax.optimization_barrier((own_stats, bn_gain, bn_shift))
    affine = jnp.stack([bn_gain, bn_shift])
    sent, back, grads_in = lax.optimization_barrier((exchanged(sent, PLANE), back, grads_in))
    stats, conv = lax.optimization_barrier((merged(sent, frames), conv))
    (product,) = call(
        moments_kernel, width, [low, inputs, high, segments, conv, own_stats], [((KERNEL, width), F32)],
        [value_copies, id_copies, column_rows],
    )
    wide = jnp.concatenate([low[: 2 * HALF], inputs, high[: 2 * HALF]])
    plain = jnp.dot(
        window_mask(frame_counts[0], first, frames, frames * devices), wide, preferred_element_type=F32
    )
    stats = gathered(stats, COLUMN)

    swished, act_grad, kept, given, norm = call(
        functools.partial(act_kernel, frames * chips), width,
        [core.reshape(1), low, inputs, high, segments, conv, back, stats, own_stats, affine, plain, product],
        [((frames, width), bf16), ((rows, width), F32), ((chips, 4, width), F32), ((chips, 4, width), F32),
         ((2, width), F32)],
        [value_copies, id_copies, column_rows, pltpu.VMEM((KERNEL, TILE), F32)],
    )
    sent, swished = lax.optimization_barrier((kept + rotated(given, "c", 1), swished))
    sent = exchanged(sent, PLANE)

    share = width // chips
    right_width = half_width // 3
    left_width = half_width - right_width
    height = share + 16
    left, right = pl.pallas_call(
        weight_kernel,
        grid_spec=pltpu.PrefetchScalarGridSpec(
            num_scalar_prefetch=1,
            grid=(4,),
            in_specs=[pl.BlockSpec((frames, width // 4), lambda i, own: (0, i))] * 2
            + [pl.BlockSpec((frames, half_width), lambda i, own: (0, own[0]))] * 2,
            out_specs=[
                pl.BlockSpec((chips // 4, share, left_width), lambda i, own: (i, 0, 0)),
                pl.BlockSpec((chips // 4, height, right_width), lambda i, own: (i, 0, 0)),
            ],
        ),
        out_shape=[
            jax.ShapeDtypeStruct((chips, share, left_width), bf16),
            jax.ShapeDtypeStruct((chips, height, right_width), bf16),
        ],
        compiler_params=PARAMS,
        cost_estimate=pl.CostEstimate(
            flops=4 * frames * width * half_width, bytes_accessed=6 * width * half_width, transcendentals=0
        ),
    )(core.reshape(1), swished, rotated(swished, "c", 1), grads_in, rotated(grads_in, "c", 1))
    block = jnp.dot(swished, proj_weight, preferred_element_type=F32).astype(bf16)
    sent, left, right = lax.optimization_barrier((sent, left, right))
    left = exchanged(left, PLANE)

    sent = jnp.sum(sent, axis=0)
    bit = 1
    while bit < lax.axis_size("z"):
        sent = sent + crossed(sent, "z", bit)
        bit *= 2
    sums = doubled(sent[3:], "c", 1)
    sums, sent, left, right = lax.optimization_barrier((sums, sent, left, right))
    right = pl.pallas_call(
        functools.partial(tap_kernel, total_rows),
        grid=(1,),
        in_specs=[cut(a.shape, 0) for a in (sent, sums, norm, affine)] + [pl.BlockSpec(memory_space=pl.ANY)],
        out_specs=pl.BlockSpec((chips, height - share, right_width), lambda i: (0, share // (height - share), 0)),
        out_shape=jax.ShapeDtypeStruct(right.shape, bf16),
        input_output_aliases={4: 0},
        compiler_params=PARAMS,
    )(sent, sums, norm, affine, right)
    right = exchanged(right, PLANE)

    (frame_grad,) = call(
        functools.partial(frame_kernel, total_rows), width,
        [segments, conv, act_grad, norm, sums, affine, tap_weight], [((frames, width), bf16)],
        [value_copies, id_copies, column_rows],
    )
    right, frame_grad, block = lax.optimization_barrier((right, frame_grad, block))
    part, tap_grad = pl.pallas_call(
        collect_kernel,
        grid=(1,),
        in_specs=[cut(left.shape, 0), cut(right.shape, 0)],
        out_specs=[cut((column, share // column, half_width), 0), cut((chips, width), 0)],
        out_shape=[
            jax.ShapeDtypeStruct((column, share // column, half_width), F32),
            jax.ShapeDtypeStruct((chips, width), F32),
        ],
        compiler_params=PARAMS,
    )(left, right)
    tap_grad = doubled(tap_grad, "c", 1)
    part = exchanged(part, COLUMN)
    part = jnp.sum(part.reshape((2, column // 2) + part.shape[1:]), axis=1)
    proj_grad = jnp.concatenate([part[0], part[1]], axis=1)
    return (block[None], frame_grad[None], tap_grad, sums[1], sums[0], proj_grad)


def solution(mesh):
    grid = Mesh(mesh.devices.reshape(4, 4, 2, -1), ("x", "y", "c", "z"))
    wide = P("z", SEQ, None)
    return jax.shard_map(
        local,
        mesh=grid,
        in_specs=(P("z", None), wide, P(), P(), P(), P(), wide),
        out_specs=(wide, wide, P(), P(), P(), P(("x", "y", "c", "z"), None)),
        check_vma=False,
    )
```

profile of v0, /device:TPU:1, one launch (start us, length us, event | category | flops | bytes accessed | tf_op | source)
XLA Modules:
  0.0 156.4 jit_solution(12818796316798608520)
XLA Ops:
  0.7 1.0 slice_bitcast_fusion
  1.7 0.8 slice_bitcast_fusion.2
  2.5 4.6 %collective-permute-start = (bf16[48,1536]{1,0:T(8,128)(2,1)S(1)}, bf16[48,1536]{1,0:T(8,128)(2,1)S(1)}, u32[]{:S(2)}, u32[]{:S(2)}) collective-permute-start(bf16[48,1536]{1,0:T(8,128)(2,1)S(1)} %pad_maximum_fusion.1), channel_id=1, source_target_pairs={{0,8},{8,16},{16,24},{24,32},{32,40},{40,48},{48,56},{56,64},{64,7... | collective-permute-start | bytes 442376 | tf_op jit(solution)/shard_map/ppermute | solution.py:27
  7.1 1.9 %collective-permute-start.1 = (bf16[48,1536]{1,0:T(8,128)(2,1)S(1)}, bf16[48,1536]{1,0:T(8,128)(2,1)S(1)}, u32[]{:S(2)}, u32[]{:S(2)}) collective-permute-start(bf16[48,1536]{1,0:T(8,128)(2,1)S(1)} %pad_maximum_fusion.2), channel_id=1, source_target_pairs={{8,0},{16,8},{24,16},{32,24},{40,32},{48,40},{56,48},{64,56},{72,6... | collective-permute-start | bytes 442376 | tf_op jit(solution)/shard_map/ppermute | solution.py:27
  9.1 0.7 copy.16
  10.3 3.3 %collective-permute-done.1.high_ref = bf16[48,1536]{1,0:T(8,128)(2,1)S(1)} collective-permute-done((bf16[48,1536]{1,0:T(8,128)(2,1)S(1)}, bf16[48,1536]{1,0:T(8,128)(2,1)S(1)}, u32[]{:S(2)}, u32[]{:S(2)}) %collective-permute-start.1) | collective-permute-done | bytes 147488 | tf_op jit(solution)/shard_map/ppermute | solution.py:27
  13.7 8.3 %shard_map.118 = (f32[224,1536]{1,0:T(8,128)S(1)}, f32[2,1536]{1,0:T(2,128)S(1)}, f32[16,2,1536]{2,1,0:T(2,128)}) custom-call(bf16[48,1536]{1,0:T(8,128)(2,1)S(1)} %collective-permute-done.low_ref, bf16[192,1536]{1,0:T(8,128)(2,1)S(1)} %bitcast.29, bf16[48,1536]{1,0:T(8,128)(2,1)S(1)} %collective-permute-done.1.high_ref, ...), custom_call_target="tpu_custom_call" | custom-call | flops 37748736 | bytes 5505024 | tf_op jit(solution)/shard_map/pallas_call | solution.py:290
  22.0 8.0 %all-to-all-start = ((f32[16,2,1536]{2,1,0:T(2,128)}), f32[16,2,1536]{2,1,0:T(2,128)S(1)}, u32[]{:S(2)}, u32[]{:S(2)}) async-start(f32[16,2,1536]{2,1,0:T(2,128)} %get-tuple-element.38), calls=%async_computation | async-start | bytes 393216 | tf_op jit(solution)/shard_map/all_to_all | solution.py:48
  30.0 5.2 %fusion.6.back_ref = f32[224,1536]{1,0:T(8,128)} fusion(bf16[1536,1536]{1,0:T(8,128)(2,1)} %param.12, bf16[16,1536]{1,0:T(8,128)(2,1)S(1)} %slice.77, bf16[192,1536]{1,0:T(8,128)(2,1)} %bitcast.7.own_grad_ref, bf16[16,1536]{1,0:T(8,128)(2,1)S(1)} %slice.76), kind=kOutput, calls=%fused_computation.7 | convolution fusion | flops 1059028992 | bytes 6782976 | tf_op jit(solution)/shard_map/dot_general | solution.py:335
  35.2 1.7 %all-to-all-done = f32[16,2,1536]{2,1,0:T(2,128)S(1)} async-done(((f32[16,2,1536]{2,1,0:T(2,128)}), f32[16,2,1536]{2,1,0:T(2,128)S(1)}, u32[]{:S(2)}, u32[]{:S(2)}) %all-to-all-start) | async-done | bytes 196640 | tf_op jit(solution)/shard_map/all_to_all | solution.py:48
  37.3 0.7 broadcast_in_dim.14
  38.0 8.6 %all-to-all-start.1 = ((f32[16,2,1536]{2,1,0:T(2,128)}), f32[16,2,1536]{2,1,0:T(2,128)S(1)}, u32[]{:S(2)}, u32[]{:S(2)}) async-start(f32[16,2,1536]{2,1,0:T(2,128)} %broadcast_in_dim.14), calls=%async_computation.1 | async-start | bytes 393216 | tf_op jit(solution)/shard_map/all_to_all | solution.py:48
  46.9 7.3 %shard_map.119.product_ref = f32[32,1536]{1,0:T(8,128)S(1)} custom-call(bf16[48,1536]{1,0:T(8,128)(2,1)S(1)} %collective-permute-done.low_ref, bf16[192,1536]{1,0:T(8,128)(2,1)S(1)} %bitcast.31, bf16[48,1536]{1,0:T(8,128)(2,1)S(1)} %collective-permute-done.1.high_ref, s32[256,128]{1,0:T(8,128)S(1)} %broadcast_in_dim.13.ids_ref, ...), custom_call_target="tpu_custom_call" | custom-call | flops 37748736 | bytes 5505024 | tf_op jit(solution)/shard_map/pallas_call | solution.py:290
  54.2 0.7 all-to-all-done.1.all_ref
  54.9 1.3 copy-done.7
  56.3 9.5 %shard_map.120 = (bf16[192,1536]{1,0:T(8,128)(2,1)}, f32[224,1536]{1,0:T(8,128)S(1)}, f32[16,4,1536]{2,1,0:T(4,128)S(1)}, f32[16,4,1536]{2,1,0:T(4,128)S(1)}, f32[2,1536]{1,0:T(2,128)S(1)}) custom-call(s32[1]{0:T(128)} %bitcast.core_ref._, bf16[48,1536]{1,0:T(8,128)(2,1)S(1)} %collective-permute-done.low_ref, bf16[192,1536]{1,0:T(8,128)(2,1)S(1)} %bitcast.32, ...), custom_call_target="tpu_custom_call" | custom-call | flops 37748736 | bytes 5505024 | tf_op jit(solution)/shard_map/pallas_call | solution.py:290
  65.8 1.1 copy-done.5
  66.9 1.0 collective-permute-start.2
  67.9 1.9 %collective-permute-done.2 = f32[16,4,1536]{2,1,0:T(4,128)S(1)} collective-permute-done((f32[16,4,1536]{2,1,0:T(4,128)S(1)}, f32[16,4,1536]{2,1,0:T(4,128)S(1)}, u32[]{:S(2)}, u32[]{:S(2)}) %collective-permute-start.2) | collective-permute-done | bytes 393248 | tf_op jit(solution)/shard_map/ppermute | solution.py:32
  69.7 0.8 add.81
  71.0 5.0 %all-to-all-start.2 = ((f32[16,4,1536]{2,1,0:T(4,128)}), f32[16,4,1536]{2,1,0:T(4,128)}, u32[]{:S(2)}, u32[]{:S(2)}) async-start(f32[16,4,1536]{2,1,0:T(4,128)} %add.81), calls=%async_computation.2 | async-start | bytes 786432 | tf_op jit(solution)/shard_map/all_to_all | solution.py:48
  76.0 3.6 %shard_map.121 = (bf16[16,96,512]{2,1,0:T(8,128)(2,1)S(1)}, bf16[16,112,256]{2,1,0:T(8,128)(2,1)S(1)}) custom-call(s32[1]{0:T(128)} %bitcast.core_ref._, bf16[192,1536]{1,0:T(8,128)(2,1)} %get-tuple-element.52.own_ref, bf16[192,1536]{1,0:T(8,128)(2,1)S(1)} %collective-permute-done.3.other_ref, bf16[192,1536]{1,0:T(8,128)(2,1)} %bitcast.7.own_grad_ref, ...), custom_call_target="tpu_custom_call" | custom-call | flops 905969664 | bytes 7077888 | tf_op jit(solution)/shard_map/pallas_call | solution.py:366
  79.6 0.9 copy-done.1
  80.5 1.1 copy-done.4
  81.6 3.7 %all-to-all-done.2 = f32[16,4,1536]{2,1,0:T(4,128)} async-done(((f32[16,4,1536]{2,1,0:T(4,128)}), f32[16,4,1536]{2,1,0:T(4,128)}, u32[]{:S(2)}, u32[]{:S(2)}) %all-to-all-start.2) | async-done | bytes 393248 | tf_op jit(solution)/shard_map/all_to_all | solution.py:48
  85.3 3.7 %all-to-all-start.3 = ((bf16[16,96,512]{2,1,0:T(8,128)(2,1)}), bf16[16,96,512]{2,1,0:T(8,128)(2,1)S(1)}, u32[]{:S(2)}, u32[]{:S(2)}) async-start(bf16[16,96,512]{2,1,0:T(8,128)(2,1)} %copy-done.4), calls=%async_computation.3 | async-start | bytes 3145728 | tf_op jit(solution)/shard_map/all_to_all | solution.py:48
  89.0 1.1 reduce_sum.58
  90.1 2.2 %collective-permute-start.5 = (f32[4,1536]{1,0:T(4,128)S(1)}, f32[4,1536]{1,0:T(4,128)S(1)}, u32[]{:S(2)}, u32[]{:S(2)}) collective-permute-start(f32[4,1536]{1,0:T(4,128)S(1)} %reduce_sum.58), channel_id=1, source_target_pairs={{0,1},{1,0},{2,3},{3,2},{4,5},{5,4},{6,7},{7,6},{8,9},{9,8},{10,11... | collective-permute-start | bytes 73736 | tf_op jit(solution)/shard_map/ppermute | solution.py:37
  92.2 1.2 collective-permute-done.5
  93.5 1.6 collective-permute-start.6
  95.0 2.4 %collective-permute-done.6 = f32[4,1536]{1,0:T(4,128)S(1)} collective-permute-done((f32[4,1536]{1,0:T(4,128)S(1)}, f32[4,1536]{1,0:T(4,128)S(1)}, u32[]{:S(2)}, u32[]{:S(2)}) %collective-permute-start.6) | collective-permute-done | bytes 24608 | tf_op jit(solution)/shard_map/ppermute | solution.py:37
  97.4 3.2 %collective-permute-start.7 = (f32[4,1536]{1,0:T(4,128)S(1)}, f32[4,1536]{1,0:T(4,128)S(1)}, u32[]{:S(2)}, u32[]{:S(2)}) collective-permute-start(f32[4,1536]{1,0:T(4,128)S(1)} %add.83), channel_id=1, source_target_pairs={{0,4},{1,5},{2,6},{3,7},{4,0},{5,1},{6,2},{7,3},{8,12},{9,13},{10,... | collective-permute-start | bytes 73736 | tf_op jit(solution)/shard_map/ppermute | solution.py:37
  100.6 3.5 %collective-permute-done.7 = f32[4,1536]{1,0:T(4,128)S(1)} collective-permute-done((f32[4,1536]{1,0:T(4,128)S(1)}, f32[4,1536]{1,0:T(4,128)S(1)}, u32[]{:S(2)}, u32[]{:S(2)}) %collective-permute-start.7) | collective-permute-done | bytes 24608 | tf_op jit(solution)/shard_map/ppermute | solution.py:37
  104.1 4.5 %collective-permute-start.8 = (f32[1,1536]{1,0:T(1,128)S(1)}, f32[1,1536]{1,0:T(1,128)S(1)}, u32[]{:S(2)}, u32[]{:S(2)}) collective-permute-start(f32[1,1536]{1,0:T(1,128)S(1)} %slice.80), channel_id=1, source_target_pairs={{0,8},{8,0},{1,9},{9,1},{2,10},{10,2},{3,11},{11,3},{4,12},{12,4},... | collective-permute-start | bytes 18440 | tf_op jit(solution)/shard_map/ppermute | solution.py:37
  108.6 0.8 collective-permute-done.8
  109.6 1.2 copy-done.2
  110.8 0.9 copy-done.3
  111.7 6.9 %all-to-all-start.4 = ((bf16[16,112,256]{2,1,0:T(8,128)(2,1)}), bf16[16,112,256]{2,1,0:T(8,128)(2,1)}, u32[]{:S(2)}, u32[]{:S(2)}) async-start(bf16[16,112,256]{2,1,0:T(8,128)(2,1)} %copy-done.3), calls=%async_computation.4 | async-start | bytes 1835008 | tf_op jit(solution)/shard_map/all_to_all | solution.py:48
  118.6 4.5 %convolution_convert_fusion = bf16[192,1536]{1,0:T(8,128)(2,1)} fusion(bf16[192,1536]{1,0:T(8,128)(2,1)} %get-tuple-element.52.own_ref, bf16[1536,1536]{1,0:T(8,128)(2,1)} %param.12), kind=kOutput, calls=%fused_computation | convolution fusion | flops 906264576 | bytes 5898240 | tf_op jit(solution)/shard_map/dot_general | solution.py:387
  123.1 7.2 %shard_map.123 = bf16[192,1536]{1,0:T(8,128)(2,1)} custom-call(s32[256,128]{1,0:T(8,128)S(1)} %broadcast_in_dim.13.ids_ref, f32[224,1536]{1,0:T(8,128)S(1)} %get-tuple-element.41.conv_ref, f32[224,1536]{1,0:T(8,128)S(1)} %copy-done.6, f32[2,1536]{1,0:T(2,128)S(1)} %get-tuple-element.61.norm_ref, f32[2,1536]{1,0:T(2,128)S(1)} %pad_maximum_fusion.6.sums_ref, ...), custom_call_target="tpu_custom_call" | custom-call | flops 37748736 | bytes 5505024 | tf_op jit(solution)/shard_map/pallas_call | solution.py:290
  130.3 2.2 %all-to-all-done.4.right_ref = bf16[16,112,256]{2,1,0:T(8,128)(2,1)} async-done(((bf16[16,112,256]{2,1,0:T(8,128)(2,1)}), bf16[16,112,256]{2,1,0:T(8,128)(2,1)}, u32[]{:S(2)}, u32[]{:S(2)}) %all-to-all-start.4) | async-done | bytes 917536 | tf_op jit(solution)/shard_map/all_to_all | solution.py:48
  132.5 2.3 %shard_map.124 = (f32[16,6,768]{2,1,0:T(8,128)}, f32[16,1536]{1,0:T(8,128)S(1)}) custom-call(bf16[16,96,512]{2,1,0:T(8,128)(2,1)S(1)} %all-to-all-done.3.left_ref, bf16[16,112,256]{2,1,0:T(8,128)(2,1)} %all-to-all-done.4.right_ref), custom_call_target="tpu_custom_call" | custom-call | tf_op jit(solution)/shard_map/pallas_call | solution.py:415
  134.8 2.8 %collective-permute-start.9 = (f32[16,1536]{1,0:T(8,128)S(1)}, f32[16,1536]{1,0:T(8,128)S(1)}, u32[]{:S(2)}, u32[]{:S(2)}) collective-permute-start(f32[16,1536]{1,0:T(8,128)S(1)} %get-tuple-element.68), channel_id=1, source_target_pairs={{0,8},{8,0},{1,9},{9,1},{2,10},{10,2},{3,11},{11,3},{4,12},{12,4},... | collective-permute-start | bytes 294920 | tf_op jit(solution)/shard_map/ppermute | solution.py:37
  137.6 0.6 slice_reduce_fusion.1
  138.2 5.1 %all-to-all-start.5 = ((f32[16,6,768]{2,1,0:T(8,128)}), f32[16,6,768]{2,1,0:T(8,128)S(1)}, u32[]{:S(2)}, u32[]{:S(2)}) async-start(f32[16,6,768]{2,1,0:T(8,128)} %get-tuple-element.69), calls=%async_computation.5 | async-start | bytes 786432 | tf_op jit(solution)/shard_map/all_to_all | solution.py:48
  143.3 0.7 pad_maximum_fusion
  144.0 11.7 %all-to-all-done.5 = f32[16,6,768]{2,1,0:T(8,128)S(1)} async-done(((f32[16,6,768]{2,1,0:T(8,128)}), f32[16,6,768]{2,1,0:T(8,128)S(1)}, u32[]{:S(2)}, u32[]{:S(2)}) %all-to-all-start.5) | async-done | bytes 294944 | tf_op jit(solution)/shard_map/all_to_all | solution.py:48
  155.7 0.6 pad_maximum_fusion.3
  (60 shorter events, 1.8 us)
Async XLA Ops:
  0.6 13.1 %copy-start = (bf16[1,192,1536]{2,1,0:T(8,128)(2,1)S(1)}, bf16[1,192,1536]{2,1,0:T(8,128)(2,1)}, u32[]{:S(2)}) copy-start(bf16[1,192,1536]{2,1,0:T(8,128)(2,1)} %param.8) | copy-start | bytes 1769476
  0.6 13.1 %copy-start.8 = (f32[32,1536]{1,0:T(8,128)S(1)}, f32[32,1536]{1,0:T(8,128)}, u32[]{:S(2)}) copy-start(f32[32,1536]{1,0:T(8,128)} %taps_ref.3) | copy-start | bytes 589828
  2.5 7.8 %collective-permute-start = (bf16[48,1536]{1,0:T(8,128)(2,1)S(1)}, bf16[48,1536]{1,0:T(8,128)(2,1)S(1)}, u32[]{:S(2)}, u32[]{:S(2)}) collective-permute-start(bf16[48,1536]{1,0:T(8,128)(2,1)S(1)} %pad_maximum_fusion.1), channel_id=1, source_target_pairs={{0,8},{8,16},{16,24},{24,32},{32,40},{40,48},{48,56},{56,64},{64,7... | collective-permute-start | bytes 442376 | tf_op jit(solution)/shard_map/ppermute | solution.py:27
  7.1 6.5 %collective-permute-start.1 = (bf16[48,1536]{1,0:T(8,128)(2,1)S(1)}, bf16[48,1536]{1,0:T(8,128)(2,1)S(1)}, u32[]{:S(2)}, u32[]{:S(2)}) collective-permute-start(bf16[48,1536]{1,0:T(8,128)(2,1)S(1)} %pad_maximum_fusion.2), channel_id=1, source_target_pairs={{8,0},{16,8},{24,16},{32,24},{40,32},{48,40},{56,48},{64,56},{72,6... | collective-permute-start | bytes 442376 | tf_op jit(solution)/shard_map/ppermute | solution.py:27
  22.0 15.0 %all-to-all-start = ((f32[16,2,1536]{2,1,0:T(2,128)}), f32[16,2,1536]{2,1,0:T(2,128)S(1)}, u32[]{:S(2)}, u32[]{:S(2)}) async-start(f32[16,2,1536]{2,1,0:T(2,128)} %get-tuple-element.38), calls=%async_computation | async-start | bytes 393216 | tf_op jit(solution)/shard_map/all_to_all | solution.py:48
  30.0 5.2 %copy-start.9 = (f32[1536]{0:T(1024)S(1)}, f32[1536]{0:T(1024)}, u32[]{:S(2)}) copy-start(f32[1536]{0:T(1024)} %param.10) | copy-start | bytes 18436
  30.0 5.2 %copy-start.10 = (f32[1536]{0:T(1024)S(1)}, f32[1536]{0:T(1024)}, u32[]{:S(2)}) copy-start(f32[1536]{0:T(1024)} %param.11) | copy-start | bytes 18436
  38.0 16.9 %all-to-all-start.1 = ((f32[16,2,1536]{2,1,0:T(2,128)}), f32[16,2,1536]{2,1,0:T(2,128)S(1)}, u32[]{:S(2)}, u32[]{:S(2)}) async-start(f32[16,2,1536]{2,1,0:T(2,128)} %broadcast_in_dim.14), calls=%async_computation.1 | async-start | bytes 393216 | tf_op jit(solution)/shard_map/all_to_all | solution.py:48
  54.9 1.3 copy-start.7
  65.8 1.1 copy-start.5
  66.9 2.9 %collective-permute-start.2 = (f32[16,4,1536]{2,1,0:T(4,128)S(1)}, f32[16,4,1536]{2,1,0:T(4,128)S(1)}, u32[]{:S(2)}, u32[]{:S(2)}) collective-permute-start(f32[16,4,1536]{2,1,0:T(4,128)S(1)} %get-tuple-element.49), channel_id=1, source_target_pairs={{0,8},{8,0},{1,9},{9,1},{2,10},{10,2},{3,11},{11,3},{4,12},{12,4},... | collective-permute-start | bytes 1179656 | tf_op jit(solution)/shard_map/ppermute | solution.py:32
  67.9 8.1 %collective-permute-start.4 = (bf16[192,1536]{1,0:T(8,128)(2,1)}, bf16[192,1536]{1,0:T(8,128)(2,1)S(1)}, u32[]{:S(2)}, u32[]{:S(2)}) collective-permute-start(bf16[192,1536]{1,0:T(8,128)(2,1)} %bitcast.7.own_grad_ref), channel_id=1, source_target_pairs={{0,8},{8,0},{1,9},{9,1},{2,10},{10,2},{3,11},{11,3},{4,12},{12,4},... | collective-permute-start | bytes 1769480 | tf_op jit(solution)/shard_map/ppermute | solution.py:32
  70.6 5.4 %collective-permute-start.3 = (bf16[192,1536]{1,0:T(8,128)(2,1)}, bf16[192,1536]{1,0:T(8,128)(2,1)S(1)}, u32[]{:S(2)}, u32[]{:S(2)}) collective-permute-start(bf16[192,1536]{1,0:T(8,128)(2,1)} %get-tuple-element.52.own_ref), channel_id=1, source_target_pairs={{0,8},{8,0},{1,9},{9,1},{2,10},{10,2},{3,11},{11,3},{4,12},{12,4},... | collective-permute-start | bytes 1769480 | tf_op jit(solution)/shard_map/ppermute | solution.py:32
  71.0 14.3 %all-to-all-start.2 = ((f32[16,4,1536]{2,1,0:T(4,128)}), f32[16,4,1536]{2,1,0:T(4,128)}, u32[]{:S(2)}, u32[]{:S(2)}) async-start(f32[16,4,1536]{2,1,0:T(4,128)} %add.81), calls=%async_computation.2 | async-start | bytes 786432 | tf_op jit(solution)/shard_map/all_to_all | solution.py:48
  79.6 0.9 copy-start.1
  80.5 1.2 copy-start.4
  85.3 24.3 %all-to-all-start.3 = ((bf16[16,96,512]{2,1,0:T(8,128)(2,1)}), bf16[16,96,512]{2,1,0:T(8,128)(2,1)S(1)}, u32[]{:S(2)}, u32[]{:S(2)}) async-start(bf16[16,96,512]{2,1,0:T(8,128)(2,1)} %copy-done.4), calls=%async_computation.3 | async-start | bytes 3145728 | tf_op jit(solution)/shard_map/all_to_all | solution.py:48
  90.1 3.4 %collective-permute-start.5 = (f32[4,1536]{1,0:T(4,128)S(1)}, f32[4,1536]{1,0:T(4,128)S(1)}, u32[]{:S(2)}, u32[]{:S(2)}) collective-permute-start(f32[4,1536]{1,0:T(4,128)S(1)} %reduce_sum.58), channel_id=1, source_target_pairs={{0,1},{1,0},{2,3},{3,2},{4,5},{5,4},{6,7},{7,6},{8,9},{9,8},{10,11... | collective-permute-start | bytes 73736 | tf_op jit(solution)/shard_map/ppermute | solution.py:37
  93.5 4.0 %collective-permute-start.6 = (f32[4,1536]{1,0:T(4,128)S(1)}, f32[4,1536]{1,0:T(4,128)S(1)}, u32[]{:S(2)}, u32[]{:S(2)}) collective-permute-start(f32[4,1536]{1,0:T(4,128)S(1)} %add.82), channel_id=1, source_target_pairs={{0,2},{1,3},{2,0},{3,1},{4,6},{5,7},{6,4},{7,5},{8,10},{9,11},{10,... | collective-permute-start | bytes 73736 | tf_op jit(solution)/shard_map/ppermute | solution.py:37
  97.4 6.7 %collective-permute-start.7 = (f32[4,1536]{1,0:T(4,128)S(1)}, f32[4,1536]{1,0:T(4,128)S(1)}, u32[]{:S(2)}, u32[]{:S(2)}) collective-permute-start(f32[4,1536]{1,0:T(4,128)S(1)} %add.83), channel_id=1, source_target_pairs={{0,4},{1,5},{2,6},{3,7},{4,0},{5,1},{6,2},{7,3},{8,12},{9,13},{10,... | collective-permute-start | bytes 73736 | tf_op jit(solution)/shard_map/ppermute | solution.py:37
  104.1 5.3 %collective-permute-start.8 = (f32[1,1536]{1,0:T(1,128)S(1)}, f32[1,1536]{1,0:T(1,128)S(1)}, u32[]{:S(2)}, u32[]{:S(2)}) collective-permute-start(f32[1,1536]{1,0:T(1,128)S(1)} %slice.80), channel_id=1, source_target_pairs={{0,8},{8,0},{1,9},{9,1},{2,10},{10,2},{3,11},{11,3},{4,12},{12,4},... | collective-permute-start | bytes 18440 | tf_op jit(solution)/shard_map/ppermute | solution.py:37
  109.6 1.2 copy-start.2
  110.8 0.9 copy-start.3
  111.7 20.8 %all-to-all-start.4 = ((bf16[16,112,256]{2,1,0:T(8,128)(2,1)}), bf16[16,112,256]{2,1,0:T(8,128)(2,1)}, u32[]{:S(2)}, u32[]{:S(2)}) async-start(bf16[16,112,256]{2,1,0:T(8,128)(2,1)} %copy-done.3), calls=%async_computation.4 | async-start | bytes 1835008 | tf_op jit(solution)/shard_map/all_to_all | solution.py:48
  118.6 4.5 %copy-start.6 = (f32[224,1536]{1,0:T(8,128)S(1)}, f32[224,1536]{1,0:T(8,128)}, u32[]{:S(2)}) copy-start(f32[224,1536]{1,0:T(8,128)} %copy-done.5) | copy-start | bytes 4128772
  134.8 8.5 %collective-permute-start.9 = (f32[16,1536]{1,0:T(8,128)S(1)}, f32[16,1536]{1,0:T(8,128)S(1)}, u32[]{:S(2)}, u32[]{:S(2)}) collective-permute-start(f32[16,1536]{1,0:T(8,128)S(1)} %get-tuple-element.68), channel_id=1, source_target_pairs={{0,8},{8,0},{1,9},{9,1},{2,10},{10,2},{3,11},{11,3},{4,12},{12,4},... | collective-permute-start | bytes 294920 | tf_op jit(solution)/shard_map/ppermute | solution.py:37
  138.2 17.5 %all-to-all-start.5 = ((f32[16,6,768]{2,1,0:T(8,128)}), f32[16,6,768]{2,1,0:T(8,128)S(1)}, u32[]{:S(2)}, u32[]{:S(2)}) async-start(f32[16,6,768]{2,1,0:T(8,128)} %get-tuple-element.69), calls=%async_computation.5 | async-start | bytes 786432 | tf_op jit(solution)/shard_map/all_to_all | solution.py:48
where the time goes:
time: 157 us; the launch traced here: 156 us
  starting transfers between devices  59.2 us (38%)
  Pallas kernels  38.2 us (24%)
  waiting for transfers between devices  33.3 us (21%)
  local copies, waits for them, and re-layouts  10.7 us (7%)
  matrix products  9.89 us (6%)
  other arithmetic  4.05 us (3%)
    all_to_all x6, starting transfers between devices, exchanged(): return lax.all_to_all(blocks, axes, 0, 0, tiled=True)  37.2 us
    pallas_call x4, Pallas kernels, call(): pl.pallas_call(kernel, grid=(width // TILE,), in_specs=[cut(a.shape, widt...  32.3 us
    all_to_all x6, waiting for transfers between devices, exchanged(): return lax.all_to_all(blocks, axes, 0, 0, tiled=True)  20.1 us
    ppermute x5, starting transfers between devices, crossed(): return lax.ppermute(value, axis, [(i, i ^ bit) for i in range(count)])  14.1 us
    ppermute x5, waiting for transfers between devices, crossed(): return lax.ppermute(value, axis, [(i, i ^ bit) for i in range(count)])  7.92 us
    unnamed x22, local copies, waits for them, and re-layouts  6.6 us
    ppermute x2, starting transfers between devices, shifted(): return lax.ppermute(value, axes, pairs)  6.52 us
    dot_general x1, matrix products, local(): lax.dot_general(grads_wide, proj_weight, (((1,), (1,)), ((), ())), prefer...  5.16 us
  transfers between devices with their start and end apart: 16, of which 12 were waited for; matrix products, arithmetic and copies ran while one was open for 9% of the time, Pallas kernels for 12%

commit v1 on v0

--- a/solution.py
+++ b/solution.py
@@ -241,7 +241,7 @@
     for all_ref, columns in ((left_ref, slice(0, left)), (right_ref, slice(left, left + size))):
         total = sum(all_ref[i, 0:rows, :].astype(F32) for i in range(all_ref.shape[0]))
         for i in range(out_ref.shape[0]):
-            out_ref[i, :, columns] = total[i * each : (i + 1) * each]
+            out_ref[i, :, columns] = total[i * each : (i + 1) * each].astype(out_ref.dtype)
     pieces = taps_ref.shape[1] // size
     for i in range(right_ref.shape[0]):
         terms = right_ref[i, rows:, :].astype(F32)
@@ -418,13 +418,13 @@
         in_specs=[cut(left.shape, 0), cut(right.shape, 0)],
         out_specs=[cut((column, share // column, half_width), 0), cut((chips, width), 0)],
         out_shape=[
-            jax.ShapeDtypeStruct((column, share // column, half_width), F32),
+            jax.ShapeDtypeStruct((column, share // column, half_width), bf16),
             jax.ShapeDtypeStruct((chips, width), F32),
         ],
         compiler_params=PARAMS,
     )(left, right)
     tap_grad = doubled(tap_grad, "c", 1)
-    part = exchanged(part, COLUMN)
+    part = exchanged(part, COLUMN).astype(F32)
     part = jnp.sum(part.reshape((2, column // 2) + part.shape[1:]), axis=1)
     proj_grad = jnp.concatenate([part[0], part[1]], axis=1)
     return (block[None], frame_grad[None], tap_grad, sums[1], sums[0], proj_grad)

time: 157 us -> 153 us (0.975)
  waiting for transfers between devices: 33.3 us -> 29.1 us
    all_to_all x6, waiting for transfers between devices: 20.1 us -> 16 us  [exchanged(): return lax.all_to_all(blocks, axes, 0, 0, tiled=True)]
where the time goes in v1:
time: 153 us; the launch traced here: 152 us
  starting transfers between devices  59.2 us (39%)
  Pallas kernels  38.2 us (25%)
  waiting for transfers between devices  29.1 us (19%)
  local copies, waits for them, and re-layouts  10.7 us (7%)
  matrix products  9.89 us (6%)
  other arithmetic  4.06 us (3%)
    all_to_all x6, starting transfers between devices, exchanged(): return lax.all_to_all(blocks, axes, 0, 0, tiled=True)  37.2 us
    pallas_call x4, Pallas kernels, call(): pl.pallas_call(kernel, grid=(width // TILE,), in_specs=[cut(a.shape, widt...  32.3 us
    all_to_all x6, waiting for transfers between devices, exchanged(): return lax.all_to_all(blocks, axes, 0, 0, tiled=True)  16 us
    ppermute x5, starting transfers between devices, crossed(): return lax.ppermute(value, axis, [(i, i ^ bit) for i in range(count)])  14.1 us
    ppermute x5, waiting for transfers between devices, crossed(): return lax.ppermute(value, axis, [(i, i ^ bit) for i in range(count)])  7.92 us
    unnamed x22, local copies, waits for them, and re-layouts  6.6 us
    ppermute x2, starting transfers between devices, shifted(): return lax.ppermute(value, axes, pairs)  6.52 us
    dot_general x1, matrix products, local(): lax.dot_general(grads_wide, proj_weight, (((1,), (1,)), ((), ())), prefer...  5.16 us
  transfers between devices with their start and end apart: 16, of which 12 were waited for; matrix products, arithmetic and copies ran while one was open for 9% of the time, Pallas kernels for 12%

profile of v1, /device:TPU:1, one launch (start us, length us, event | category | flops | bytes accessed | tf_op | source)
XLA Modules:
  0.0 152.1 jit_solution(10059152063243047953)
XLA Ops:
  0.7 1.0 slice_bitcast_fusion
  1.7 0.8 slice_bitcast_fusion.2
  2.5 4.6 %collective-permute-start = (bf16[48,1536]{1,0:T(8,128)(2,1)S(1)}, bf16[48,1536]{1,0:T(8,128)(2,1)S(1)}, u32[]{:S(2)}, u32[]{:S(2)}) collective-permute-start(bf16[48,1536]{1,0:T(8,128)(2,1)S(1)} %pad_maximum_fusion.1), channel_id=1, source_target_pairs={{0,8},{8,16},{16,24},{24,32},{32,40},{40,48},{48,56},{56,64},{64,7... | collective-permute-start | bytes 442376 | tf_op jit(solution)/shard_map/ppermute | solution.py:27
  7.1 1.9 %collective-permute-start.1 = (bf16[48,1536]{1,0:T(8,128)(2,1)S(1)}, bf16[48,1536]{1,0:T(8,128)(2,1)S(1)}, u32[]{:S(2)}, u32[]{:S(2)}) collective-permute-start(bf16[48,1536]{1,0:T(8,128)(2,1)S(1)} %pad_maximum_fusion.2), channel_id=1, source_target_pairs={{8,0},{16,8},{24,16},{32,24},{40,32},{48,40},{56,48},{64,56},{72,6... | collective-permute-start | bytes 442376 | tf_op jit(solution)/shard_map/ppermute | solution.py:27
  9.1 0.7 copy.16
  10.3 3.3 %collective-permute-done.1.high_ref = bf16[48,1536]{1,0:T(8,128)(2,1)S(1)} collective-permute-done((bf16[48,1536]{1,0:T(8,128)(2,1)S(1)}, bf16[48,1536]{1,0:T(8,128)(2,1)S(1)}, u32[]{:S(2)}, u32[]{:S(2)}) %collective-permute-start.1) | collective-permute-done | bytes 147488 | tf_op jit(solution)/shard_map/ppermute | solution.py:27
  13.7 8.3 %shard_map.118 = (f32[224,1536]{1,0:T(8,128)S(1)}, f32[2,1536]{1,0:T(2,128)S(1)}, f32[16,2,1536]{2,1,0:T(2,128)}) custom-call(bf16[48,1536]{1,0:T(8,128)(2,1)S(1)} %collective-permute-done.low_ref, bf16[192,1536]{1,0:T(8,128)(2,1)S(1)} %bitcast.30, bf16[48,1536]{1,0:T(8,128)(2,1)S(1)} %collective-permute-done.1.high_ref, ...), custom_call_target="tpu_custom_call" | custom-call | flops 37748736 | bytes 5505024 | tf_op jit(solution)/shard_map/pallas_call | solution.py:290
  22.0 8.0 %all-to-all-start = ((f32[16,2,1536]{2,1,0:T(2,128)}), f32[16,2,1536]{2,1,0:T(2,128)S(1)}, u32[]{:S(2)}, u32[]{:S(2)}) async-start(f32[16,2,1536]{2,1,0:T(2,128)} %get-tuple-element.38), calls=%async_computation | async-start | bytes 393216 | tf_op jit(solution)/shard_map/all_to_all | solution.py:48
  30.0 5.2 %fusion.6.back_ref = f32[224,1536]{1,0:T(8,128)} fusion(bf16[1536,1536]{1,0:T(8,128)(2,1)} %param.12, bf16[16,1536]{1,0:T(8,128)(2,1)S(1)} %slice.77, bf16[192,1536]{1,0:T(8,128)(2,1)} %bitcast.7.own_grad_ref, bf16[16,1536]{1,0:T(8,128)(2,1)S(1)} %slice.76), kind=kOutput, calls=%fused_computation.7 | convolution fusion | flops 1059028992 | bytes 6782976 | tf_op jit(solution)/shard_map/dot_general | solution.py:335
  35.2 1.7 %all-to-all-done = f32[16,2,1536]{2,1,0:T(2,128)S(1)} async-done(((f32[16,2,1536]{2,1,0:T(2,128)}), f32[16,2,1536]{2,1,0:T(2,128)S(1)}, u32[]{:S(2)}, u32[]{:S(2)}) %all-to-all-start) | async-done | bytes 196640 | tf_op jit(solution)/shard_map/all_to_all | solution.py:48
  37.3 0.7 broadcast_in_dim.14
  38.0 8.6 %all-to-all-start.1 = ((f32[16,2,1536]{2,1,0:T(2,128)}), f32[16,2,1536]{2,1,0:T(2,128)S(1)}, u32[]{:S(2)}, u32[]{:S(2)}) async-start(f32[16,2,1536]{2,1,0:T(2,128)} %broadcast_in_dim.14), calls=%async_computation.1 | async-start | bytes 393216 | tf_op jit(solution)/shard_map/all_to_all | solution.py:48
  46.9 7.3 %shard_map.119.product_ref = f32[32,1536]{1,0:T(8,128)S(1)} custom-call(bf16[48,1536]{1,0:T(8,128)(2,1)S(1)} %collective-permute-done.low_ref, bf16[192,1536]{1,0:T(8,128)(2,1)S(1)} %bitcast.32, bf16[48,1536]{1,0:T(8,128)(2,1)S(1)} %collective-permute-done.1.high_ref, s32[256,128]{1,0:T(8,128)S(1)} %broadcast_in_dim.13.ids_ref, ...), custom_call_target="tpu_custom_call" | custom-call | flops 37748736 | bytes 5505024 | tf_op jit(solution)/shard_map/pallas_call | solution.py:290
  54.2 0.7 all-to-all-done.1.all_ref
  54.9 1.3 copy-done.7
  56.3 9.5 %shard_map.120 = (bf16[192,1536]{1,0:T(8,128)(2,1)}, f32[224,1536]{1,0:T(8,128)S(1)}, f32[16,4,1536]{2,1,0:T(4,128)S(1)}, f32[16,4,1536]{2,1,0:T(4,128)S(1)}, f32[2,1536]{1,0:T(2,128)S(1)}) custom-call(s32[1]{0:T(128)} %bitcast.core_ref._, bf16[48,1536]{1,0:T(8,128)(2,1)S(1)} %collective-permute-done.low_ref, bf16[192,1536]{1,0:T(8,128)(2,1)S(1)} %bitcast.33, ...), custom_call_target="tpu_custom_call" | custom-call | flops 37748736 | bytes 5505024 | tf_op jit(solution)/shard_map/pallas_call | solution.py:290
  65.8 1.1 copy-done.5
  66.9 1.0 collective-permute-start.2
  67.9 1.9 %collective-permute-done.2 = f32[16,4,1536]{2,1,0:T(4,128)S(1)} collective-permute-done((f32[16,4,1536]{2,1,0:T(4,128)S(1)}, f32[16,4,1536]{2,1,0:T(4,128)S(1)}, u32[]{:S(2)}, u32[]{:S(2)}) %collective-permute-start.2) | collective-permute-done | bytes 393248 | tf_op jit(solution)/shard_map/ppermute | solution.py:32
  69.7 0.8 add.81
  71.0 5.0 %all-to-all-start.2 = ((f32[16,4,1536]{2,1,0:T(4,128)}), f32[16,4,1536]{2,1,0:T(4,128)}, u32[]{:S(2)}, u32[]{:S(2)}) async-start(f32[16,4,1536]{2,1,0:T(4,128)} %add.81), calls=%async_computation.2 | async-start | bytes 786432 | tf_op jit(solution)/shard_map/all_to_all | solution.py:48
  76.0 3.6 %shard_map.121 = (bf16[16,96,512]{2,1,0:T(8,128)(2,1)S(1)}, bf16[16,112,256]{2,1,0:T(8,128)(2,1)S(1)}) custom-call(s32[1]{0:T(128)} %bitcast.core_ref._, bf16[192,1536]{1,0:T(8,128)(2,1)} %get-tuple-element.52.own_ref, bf16[192,1536]{1,0:T(8,128)(2,1)S(1)} %collective-permute-done.3.other_ref, bf16[192,1536]{1,0:T(8,128)(2,1)} %bitcast.7.own_grad_ref, ...), custom_call_target="tpu_custom_call" | custom-call | flops 905969664 | bytes 7077888 | tf_op jit(solution)/shard_map/pallas_call | solution.py:366
  79.6 0.9 copy-done.1
  80.5 1.1 copy-done.4
  81.6 3.7 %all-to-all-done.2 = f32[16,4,1536]{2,1,0:T(4,128)} async-done(((f32[16,4,1536]{2,1,0:T(4,128)}), f32[16,4,1536]{2,1,0:T(4,128)}, u32[]{:S(2)}, u32[]{:S(2)}) %all-to-all-start.2) | async-done | bytes 393248 | tf_op jit(solution)/shard_map/all_to_all | solution.py:48
  85.3 3.7 %all-to-all-start.3 = ((bf16[16,96,512]{2,1,0:T(8,128)(2,1)}), bf16[16,96,512]{2,1,0:T(8,128)(2,1)S(1)}, u32[]{:S(2)}, u32[]{:S(2)}) async-start(bf16[16,96,512]{2,1,0:T(8,128)(2,1)} %copy-done.4), calls=%async_computation.3 | async-start | bytes 3145728 | tf_op jit(solution)/shard_map/all_to_all | solution.py:48
  89.0 1.1 reduce_sum.58
  90.1 2.2 %collective-permute-start.5 = (f32[4,1536]{1,0:T(4,128)S(1)}, f32[4,1536]{1,0:T(4,128)S(1)}, u32[]{:S(2)}, u32[]{:S(2)}) collective-permute-start(f32[4,1536]{1,0:T(4,128)S(1)} %reduce_sum.58), channel_id=1, source_target_pairs={{0,1},{1,0},{2,3},{3,2},{4,5},{5,4},{6,7},{7,6},{8,9},{9,8},{10,11... | collective-permute-start | bytes 73736 | tf_op jit(solution)/shard_map/ppermute | solution.py:37
  92.2 1.2 collective-permute-done.5
  93.5 1.6 %collective-permute-start.6 = (f32[4,1536]{1,0:T(4,128)S(1)}, f32[4,1536]{1,0:T(4,128)S(1)}, u32[]{:S(2)}, u32[]{:S(2)}) collective-permute-start(f32[4,1536]{1,0:T(4,128)S(1)} %add.82), channel_id=1, source_target_pairs={{0,2},{1,3},{2,0},{3,1},{4,6},{5,7},{6,4},{7,5},{8,10},{9,11},{10,... | collective-permute-start | bytes 73736 | tf_op jit(solution)/shard_map/ppermute | solution.py:37
  95.0 2.4 %collective-permute-done.6 = f32[4,1536]{1,0:T(4,128)S(1)} collective-permute-done((f32[4,1536]{1,0:T(4,128)S(1)}, f32[4,1536]{1,0:T(4,128)S(1)}, u32[]{:S(2)}, u32[]{:S(2)}) %collective-permute-start.6) | collective-permute-done | bytes 24608 | tf_op jit(solution)/shard_map/ppermute | solution.py:37
  97.4 3.2 %collective-permute-start.7 = (f32[4,1536]{1,0:T(4,128)S(1)}, f32[4,1536]{1,0:T(4,128)S(1)}, u32[]{:S(2)}, u32[]{:S(2)}) collective-permute-start(f32[4,1536]{1,0:T(4,128)S(1)} %add.83), channel_id=1, source_target_pairs={{0,4},{1,5},{2,6},{3,7},{4,0},{5,1},{6,2},{7,3},{8,12},{9,13},{10,... | collective-permute-start | bytes 73736 | tf_op jit(solution)/shard_map/ppermute | solution.py:37
  100.6 3.5 %collective-permute-done.7 = f32[4,1536]{1,0:T(4,128)S(1)} collective-permute-done((f32[4,1536]{1,0:T(4,128)S(1)}, f32[4,1536]{1,0:T(4,128)S(1)}, u32[]{:S(2)}, u32[]{:S(2)}) %collective-permute-start.7) | collective-permute-done | bytes 24608 | tf_op jit(solution)/shard_map/ppermute | solution.py:37
  104.1 4.5 %collective-permute-start.8 = (f32[1,1536]{1,0:T(1,128)S(1)}, f32[1,1536]{1,0:T(1,128)S(1)}, u32[]{:S(2)}, u32[]{:S(2)}) collective-permute-start(f32[1,1536]{1,0:T(1,128)S(1)} %slice.80), channel_id=1, source_target_pairs={{0,8},{8,0},{1,9},{9,1},{2,10},{10,2},{3,11},{11,3},{4,12},{12,4},... | collective-permute-start | bytes 18440 | tf_op jit(solution)/shard_map/ppermute | solution.py:37
  108.6 0.8 collective-permute-done.8
  109.6 1.2 copy-done.2
  110.8 0.9 copy-done.3
  111.7 6.9 %all-to-all-start.4 = ((bf16[16,112,256]{2,1,0:T(8,128)(2,1)}), bf16[16,112,256]{2,1,0:T(8,128)(2,1)}, u32[]{:S(2)}, u32[]{:S(2)}) async-start(bf16[16,112,256]{2,1,0:T(8,128)(2,1)} %copy-done.3), calls=%async_computation.4 | async-start | bytes 1835008 | tf_op jit(solution)/shard_map/all_to_all | solution.py:48
  118.6 4.5 %convolution_convert_fusion = bf16[192,1536]{1,0:T(8,128)(2,1)} fusion(bf16[192,1536]{1,0:T(8,128)(2,1)} %get-tuple-element.52.own_ref, bf16[1536,1536]{1,0:T(8,128)(2,1)} %param.12), kind=kOutput, calls=%fused_computation | convolution fusion | flops 906264576 | bytes 5898240 | tf_op jit(solution)/shard_map/dot_general | solution.py:387
  123.1 7.2 %shard_map.123 = bf16[192,1536]{1,0:T(8,128)(2,1)} custom-call(s32[256,128]{1,0:T(8,128)S(1)} %broadcast_in_dim.13.ids_ref, f32[224,1536]{1,0:T(8,128)S(1)} %get-tuple-element.41.conv_ref, f32[224,1536]{1,0:T(8,128)S(1)} %copy-done.6, f32[2,1536]{1,0:T(2,128)S(1)} %get-tuple-element.61.norm_ref, f32[2,1536]{1,0:T(2,128)S(1)} %pad_maximum_fusion.6.sums_ref, ...), custom_call_target="tpu_custom_call" | custom-call | flops 37748736 | bytes 5505024 | tf_op jit(solution)/shard_map/pallas_call | solution.py:290
  130.3 2.2 %all-to-all-done.4.right_ref = bf16[16,112,256]{2,1,0:T(8,128)(2,1)} async-done(((bf16[16,112,256]{2,1,0:T(8,128)(2,1)}), bf16[16,112,256]{2,1,0:T(8,128)(2,1)}, u32[]{:S(2)}, u32[]{:S(2)}) %all-to-all-start.4) | async-done | bytes 917536 | tf_op jit(solution)/shard_map/all_to_all | solution.py:48
  132.5 2.2 %shard_map.124 = (bf16[16,6,768]{2,1,0:T(8,128)(2,1)}, f32[16,1536]{1,0:T(8,128)S(1)}) custom-call(bf16[16,96,512]{2,1,0:T(8,128)(2,1)S(1)} %all-to-all-done.3.left_ref, bf16[16,112,256]{2,1,0:T(8,128)(2,1)} %all-to-all-done.4.right_ref), custom_call_target="tpu_custom_call" | custom-call | tf_op jit(solution)/shard_map/pallas_call | solution.py:415
  134.7 2.8 %collective-permute-start.9 = (f32[16,1536]{1,0:T(8,128)S(1)}, f32[16,1536]{1,0:T(8,128)S(1)}, u32[]{:S(2)}, u32[]{:S(2)}) collective-permute-start(f32[16,1536]{1,0:T(8,128)S(1)} %get-tuple-element.68), channel_id=1, source_target_pairs={{0,8},{8,0},{1,9},{9,1},{2,10},{10,2},{3,11},{11,3},{4,12},{12,4},... | collective-permute-start | bytes 294920 | tf_op jit(solution)/shard_map/ppermute | solution.py:37
  137.5 0.6 slice_reduce_fusion.1
  138.1 5.1 %all-to-all-start.5 = ((bf16[16,6,768]{2,1,0:T(8,128)(2,1)}), bf16[16,6,768]{2,1,0:T(8,128)(2,1)S(1)}, u32[]{:S(2)}, u32[]{:S(2)}) async-start(bf16[16,6,768]{2,1,0:T(8,128)(2,1)} %get-tuple-element.69), calls=%async_computation.5 | async-start | bytes 393216 | tf_op jit(solution)/shard_map/all_to_all | solution.py:48
  143.2 0.7 pad_maximum_fusion
  143.9 7.6 %all-to-all-done.5 = bf16[16,6,768]{2,1,0:T(8,128)(2,1)S(1)} async-done(((bf16[16,6,768]{2,1,0:T(8,128)(2,1)}), bf16[16,6,768]{2,1,0:T(8,128)(2,1)S(1)}, u32[]{:S(2)}, u32[]{:S(2)}) %all-to-all-start.5) | async-done | bytes 147488 | tf_op jit(solution)/shard_map/all_to_all | solution.py:48
  151.5 0.6 pad_maximum_fusion.3
  (60 shorter events, 1.8 us)
Async XLA Ops:
  0.6 13.1 %copy-start = (bf16[1,192,1536]{2,1,0:T(8,128)(2,1)S(1)}, bf16[1,192,1536]{2,1,0:T(8,128)(2,1)}, u32[]{:S(2)}) copy-start(bf16[1,192,1536]{2,1,0:T(8,128)(2,1)} %param.8) | copy-start | bytes 1769476
  0.6 13.1 %copy-start.8 = (f32[32,1536]{1,0:T(8,128)S(1)}, f32[32,1536]{1,0:T(8,128)}, u32[]{:S(2)}) copy-start(f32[32,1536]{1,0:T(8,128)} %taps_ref.3) | copy-start | bytes 589828
  2.5 7.8 %collective-permute-start = (bf16[48,1536]{1,0:T(8,128)(2,1)S(1)}, bf16[48,1536]{1,0:T(8,128)(2,1)S(1)}, u32[]{:S(2)}, u32[]{:S(2)}) collective-permute-start(bf16[48,1536]{1,0:T(8,128)(2,1)S(1)} %pad_maximum_fusion.1), channel_id=1, source_target_pairs={{0,8},{8,16},{16,24},{24,32},{32,40},{40,48},{48,56},{56,64},{64,7... | collective-permute-start | bytes 442376 | tf_op jit(solution)/shard_map/ppermute | solution.py:27
  7.1 6.5 %collective-permute-start.1 = (bf16[48,1536]{1,0:T(8,128)(2,1)S(1)}, bf16[48,1536]{1,0:T(8,128)(2,1)S(1)}, u32[]{:S(2)}, u32[]{:S(2)}) collective-permute-start(bf16[48,1536]{1,0:T(8,128)(2,1)S(1)} %pad_maximum_fusion.2), channel_id=1, source_target_pairs={{8,0},{16,8},{24,16},{32,24},{40,32},{48,40},{56,48},{64,56},{72,6... | collective-permute-start | bytes 442376 | tf_op jit(solution)/shard_map/ppermute | solution.py:27
  22.0 15.0 %all-to-all-start = ((f32[16,2,1536]{2,1,0:T(2,128)}), f32[16,2,1536]{2,1,0:T(2,128)S(1)}, u32[]{:S(2)}, u32[]{:S(2)}) async-start(f32[16,2,1536]{2,1,0:T(2,128)} %get-tuple-element.38), calls=%async_computation | async-start | bytes 393216 | tf_op jit(solution)/shard_map/all_to_all | solution.py:48
  30.0 5.2 %copy-start.9 = (f32[1536]{0:T(1024)S(1)}, f32[1536]{0:T(1024)}, u32[]{:S(2)}) copy-start(f32[1536]{0:T(1024)} %param.10) | copy-start | bytes 18436
  30.0 5.2 %copy-start.10 = (f32[1536]{0:T(1024)S(1)}, f32[1536]{0:T(1024)}, u32[]{:S(2)}) copy-start(f32[1536]{0:T(1024)} %param.11) | copy-start | bytes 18436
  38.0 16.9 %all-to-all-start.1 = ((f32[16,2,1536]{2,1,0:T(2,128)}), f32[16,2,1536]{2,1,0:T(2,128)S(1)}, u32[]{:S(2)}, u32[]{:S(2)}) async-start(f32[16,2,1536]{2,1,0:T(2,128)} %broadcast_in_dim.14), calls=%async_computation.1 | async-start | bytes 393216 | tf_op jit(solution)/shard_map/all_to_all | solution.py:48
  54.9 1.3 copy-start.7
  65.8 1.1 copy-start.5
  66.9 2.9 %collective-permute-start.2 = (f32[16,4,1536]{2,1,0:T(4,128)S(1)}, f32[16,4,1536]{2,1,0:T(4,128)S(1)}, u32[]{:S(2)}, u32[]{:S(2)}) collective-permute-start(f32[16,4,1536]{2,1,0:T(4,128)S(1)} %get-tuple-element.49), channel_id=1, source_target_pairs={{0,8},{8,0},{1,9},{9,1},{2,10},{10,2},{3,11},{11,3},{4,12},{12,4},... | collective-permute-start | bytes 1179656 | tf_op jit(solution)/shard_map/ppermute | solution.py:32
  67.9 8.1 %collective-permute-start.4 = (bf16[192,1536]{1,0:T(8,128)(2,1)}, bf16[192,1536]{1,0:T(8,128)(2,1)S(1)}, u32[]{:S(2)}, u32[]{:S(2)}) collective-permute-start(bf16[192,1536]{1,0:T(8,128)(2,1)} %bitcast.7.own_grad_ref), channel_id=1, source_target_pairs={{0,8},{8,0},{1,9},{9,1},{2,10},{10,2},{3,11},{11,3},{4,12},{12,4},... | collective-permute-start | bytes 1769480 | tf_op jit(solution)/shard_map/ppermute | solution.py:32
  70.6 5.4 %collective-permute-start.3 = (bf16[192,1536]{1,0:T(8,128)(2,1)}, bf16[192,1536]{1,0:T(8,128)(2,1)S(1)}, u32[]{:S(2)}, u32[]{:S(2)}) collective-permute-start(bf16[192,1536]{1,0:T(8,128)(2,1)} %get-tuple-element.52.own_ref), channel_id=1, source_target_pairs={{0,8},{8,0},{1,9},{9,1},{2,10},{10,2},{3,11},{11,3},{4,12},{12,4},... | collective-permute-start | bytes 1769480 | tf_op jit(solution)/shard_map/ppermute | solution.py:32
  71.0 14.3 %all-to-all-start.2 = ((f32[16,4,1536]{2,1,0:T(4,128)}), f32[16,4,1536]{2,1,0:T(4,128)}, u32[]{:S(2)}, u32[]{:S(2)}) async-start(f32[16,4,1536]{2,1,0:T(4,128)} %add.81), calls=%async_computation.2 | async-start | bytes 786432 | tf_op jit(solution)/shard_map/all_to_all | solution.py:48
  79.6 0.9 copy-start.1
  80.5 1.2 copy-start.4
  85.3 24.3 %all-to-all-start.3 = ((bf16[16,96,512]{2,1,0:T(8,128)(2,1)}), bf16[16,96,512]{2,1,0:T(8,128)(2,1)S(1)}, u32[]{:S(2)}, u32[]{:S(2)}) async-start(bf16[16,96,512]{2,1,0:T(8,128)(2,1)} %copy-done.4), calls=%async_computation.3 | async-start | bytes 3145728 | tf_op jit(solution)/shard_map/all_to_all | solution.py:48
  90.1 3.4 %collective-permute-start.5 = (f32[4,1536]{1,0:T(4,128)S(1)}, f32[4,1536]{1,0:T(4,128)S(1)}, u32[]{:S(2)}, u32[]{:S(2)}) collective-permute-start(f32[4,1536]{1,0:T(4,128)S(1)} %reduce_sum.58), channel_id=1, source_target_pairs={{0,1},{1,0},{2,3},{3,2},{4,5},{5,4},{6,7},{7,6},{8,9},{9,8},{10,11... | collective-permute-start | bytes 73736 | tf_op jit(solution)/shard_map/ppermute | solution.py:37
  93.5 4.0 %collective-permute-start.6 = (f32[4,1536]{1,0:T(4,128)S(1)}, f32[4,1536]{1,0:T(4,128)S(1)}, u32[]{:S(2)}, u32[]{:S(2)}) collective-permute-start(f32[4,1536]{1,0:T(4,128)S(1)} %add.82), channel_id=1, source_target_pairs={{0,2},{1,3},{2,0},{3,1},{4,6},{5,7},{6,4},{7,5},{8,10},{9,11},{10,... | collective-permute-start | bytes 73736 | tf_op jit(solution)/shard_map/ppermute | solution.py:37
  97.4 6.7 %collective-permute-start.7 = (f32[4,1536]{1,0:T(4,128)S(1)}, f32[4,1536]{1,0:T(4,128)S(1)}, u32[]{:S(2)}, u32[]{:S(2)}) collective-permute-start(f32[4,1536]{1,0:T(4,128)S(1)} %add.83), channel_id=1, source_target_pairs={{0,4},{1,5},{2,6},{3,7},{4,0},{5,1},{6,2},{7,3},{8,12},{9,13},{10,... | collective-permute-start | bytes 73736 | tf_op jit(solution)/shard_map/ppermute | solution.py:37
  104.1 5.3 %collective-permute-start.8 = (f32[1,1536]{1,0:T(1,128)S(1)}, f32[1,1536]{1,0:T(1,128)S(1)}, u32[]{:S(2)}, u32[]{:S(2)}) collective-permute-start(f32[1,1536]{1,0:T(1,128)S(1)} %slice.80), channel_id=1, source_target_pairs={{0,8},{8,0},{1,9},{9,1},{2,10},{10,2},{3,11},{11,3},{4,12},{12,4},... | collective-permute-start | bytes 18440 | tf_op jit(solution)/shard_map/ppermute | solution.py:37
  109.6 1.2 copy-start.2
  110.8 0.9 copy-start.3
  111.7 20.8 %all-to-all-start.4 = ((bf16[16,112,256]{2,1,0:T(8,128)(2,1)}), bf16[16,112,256]{2,1,0:T(8,128)(2,1)}, u32[]{:S(2)}, u32[]{:S(2)}) async-start(bf16[16,112,256]{2,1,0:T(8,128)(2,1)} %copy-done.3), calls=%async_computation.4 | async-start | bytes 1835008 | tf_op jit(solution)/shard_map/all_to_all | solution.py:48
  118.6 4.5 %copy-start.6 = (f32[224,1536]{1,0:T(8,128)S(1)}, f32[224,1536]{1,0:T(8,128)}, u32[]{:S(2)}) copy-start(f32[224,1536]{1,0:T(8,128)} %copy-done.5) | copy-start | bytes 4128772
  134.7 8.5 %collective-permute-start.9 = (f32[16,1536]{1,0:T(8,128)S(1)}, f32[16,1536]{1,0:T(8,128)S(1)}, u32[]{:S(2)}, u32[]{:S(2)}) collective-permute-start(f32[16,1536]{1,0:T(8,128)S(1)} %get-tuple-element.68), channel_id=1, source_target_pairs={{0,8},{8,0},{1,9},{9,1},{2,10},{10,2},{3,11},{11,3},{4,12},{12,4},... | collective-permute-start | bytes 294920 | tf_op jit(solution)/shard_map/ppermute | solution.py:37
  138.1 13.3 %all-to-all-start.5 = ((bf16[16,6,768]{2,1,0:T(8,128)(2,1)}), bf16[16,6,768]{2,1,0:T(8,128)(2,1)S(1)}, u32[]{:S(2)}, u32[]{:S(2)}) async-start(bf16[16,6,768]{2,1,0:T(8,128)(2,1)} %get-tuple-element.69), calls=%async_computation.5 | async-start | bytes 393216 | tf_op jit(solution)/shard_map/all_to_all | solution.py:48

commit v2 on v1

--- a/solution.py
+++ b/solution.py
@@ -16,7 +16,7 @@
 LANES = 128
 TILE = 512
 SUB = 8
-BLOCKS = 4
+WIDEST = 8
 GROUP = 4
 F32 = jnp.float32
 
@@ -87,55 +87,62 @@
     return [tiles[t : t + GROUP] for t in range(0, len(tiles), GROUP)]
 
 
+def blocks_of(rows):
+    count = rows // SUB
+    return max(b for b in range(1, WIDEST + 1) if count % b == 0)
+
+
 def convolve(ids_ref, ids, copies, taps_ref, out_ref, rows, centre, tap_of, id_shift):
+    blocks = blocks_of(rows)
     offsets = [o for o in range(KERNEL + 1) if 0 <= tap_of(o) < KERNEL]
     for tiles in lane_groups():
         def step(j, carry, tiles=tiles):
-            base = pl.multiple_of(j * SUB * BLOCKS, SUB * BLOCKS)
-            own = [ids_ref[pl.ds(base + i * SUB + centre, SUB), :] for i in range(BLOCKS)]
-            totals = [[jnp.zeros((SUB, LANES), F32) for _ in tiles] for _ in range(BLOCKS)]
+            base = pl.multiple_of(j * SUB * blocks, SUB * blocks)
+            own = [ids_ref[pl.ds(base + i * SUB + centre, SUB), :] for i in range(blocks)]
+            totals = [[jnp.zeros((SUB, LANES), F32) for _ in tiles] for _ in range(blocks)]
             for low in range(SUB):
                 steps = [o // SUB for o in offsets if o % SUB == low]
-                reads = range(min(steps), max(steps) + BLOCKS)
+                reads = range(min(steps), max(steps) + blocks)
                 near = {i: ids[low, pl.ds(base + i * SUB + id_shift, SUB), :] for i in reads}
-                keep = {(a, i): near[a + i] == own[i] for a in steps for i in range(BLOCKS)}
+                keep = {(a, i): near[a + i] == own[i] for a in steps for i in range(blocks)}
                 for t, lanes in enumerate(tiles):
                     value = {i: copies[low, pl.ds(base + i * SUB, SUB), lanes] for i in reads}
                     for a in steps:
                         tap = taps_ref[pl.ds(tap_of(a * SUB + low), 1), lanes]
-                        for i in range(BLOCKS):
+                        for i in range(blocks):
                             term = jnp.where(keep[a, i], value[a + i], 0.0)
                             totals[i][t] = totals[i][t] + tap * term
-            for i in range(BLOCKS):
+            for i in range(blocks):
                 for t, lanes in enumerate(tiles):
                     out_ref[pl.ds(base + i * SUB, SUB), lanes] = totals[i][t]
             return carry
 
-        lax.fori_loop(0, rows // (SUB * BLOCKS), step, 0)
+        lax.fori_loop(0, rows // (SUB * blocks), step, 0)
 
 
 def correlate(grad_ref, ids_ref, ids, copies, rows, first, out_ref):
+    blocks = blocks_of(rows)
     steps = range(KERNEL // SUB)
     for tiles in lane_groups():
         for low in range(SUB):
             def step(j, sums, tiles=tiles, low=low):
-                base = pl.multiple_of(j * SUB * BLOCKS, SUB * BLOCKS)
-                reads = range(len(steps) + BLOCKS - 1)
-                own = [ids_ref[pl.ds(base + i * SUB + first + HALF, SUB), :] for i in range(BLOCKS)]
+                base = pl.multiple_of(j * SUB * blocks, SUB * blocks)
+                reads = range(len(steps) + blocks - 1)
+                own = [ids_ref[pl.ds(base + i * SUB + first + HALF, SUB), :] for i in range(blocks)]
                 near = [ids[low, pl.ds(base + i * SUB + first, SUB), :] for i in reads]
-                keep = {(a, i): near[a + i] == own[i] for a in steps for i in range(BLOCKS)}
+                keep = {(a, i): near[a + i] == own[i] for a in steps for i in range(blocks)}
                 out = list(sums)
                 for t, lanes in enumerate(tiles):
                     value = [copies[low, pl.ds(base + i * SUB + first, SUB), lanes] for i in reads]
-                    grads = [grad_ref[pl.ds(base + i * SUB, SUB), lanes] for i in range(BLOCKS)]
+                    grads = [grad_ref[pl.ds(base + i * SUB, SUB), lanes] for i in range(blocks)]
                     for a in steps:
                         at = t * len(steps) + a
-                        for i in range(BLOCKS):
+                        for i in range(blocks):
                             out[at] = out[at] + jnp.where(keep[a, i], value[a + i], 0.0) * grads[i]
                 return tuple(out)
 
             start = tuple(jnp.zeros((SUB, LANES), F32) for _ in range(len(steps) * len(tiles)))
-            sums = lax.fori_loop(0, rows // (SUB * BLOCKS), step, start)
+            sums = lax.fori_loop(0, rows // (SUB * blocks), step, start)
             for t, lanes in enumerate(tiles):
                 for a in steps:
                     total = jnp.sum(sums[t * len(steps) + a], axis=0, keepdims=True)

time: 153 us -> 153 us (level)
  transfers between devices with their start and end apart: 16 -> 16, of which waited for: 12 -> 11; matrix products, arithmetic and copies ran while one was open for 9% -> 9% of each run, Pallas kernels for 12% -> 12%
where the time goes in v2:
time: 153 us; the launch traced here: 152 us
  starting transfers between devices  59.3 us (39%)
  Pallas kernels  37.8 us (25%)
  waiting for transfers between devices  29.3 us (19%)
  local copies, waits for them, and re-layouts  10.7 us (7%)
  matrix products  9.88 us (6%)
  other arithmetic  4.06 us (3%)
    all_to_all x6, starting transfers between devices, exchanged(): return lax.all_to_all(blocks, axes, 0, 0, tiled=True)  37.1 us
    pallas_call x4, Pallas kernels, call(): pl.pallas_call(kernel, grid=(width // TILE,), in_specs=[cut(a.shape, widt...  32 us
    all_to_all x6, waiting for transfers between devices, exchanged(): return lax.all_to_all(blocks, axes, 0, 0, tiled=True)  16.1 us
    ppermute x5, starting transfers between devices, crossed(): return lax.ppermute(value, axis, [(i, i ^ bit) for i in range(count)])  14.3 us
    ppermute x5, waiting for transfers between devices, crossed(): return lax.ppermute(value, axis, [(i, i ^ bit) for i in range(count)])  8.01 us
    unnamed x22, local copies, waits for them, and re-layouts  6.59 us
    ppermute x2, starting transfers between devices, shifted(): return lax.ppermute(value, axes, pairs)  6.52 us
    dot_general x1, matrix products, local(): lax.dot_general(grads_wide, proj_weight, (((1,), (1,)), ((), ())), prefer...  5.15 us
  transfers between devices with their start and end apart: 16, of which 11 were waited for; matrix products, arithmetic and copies ran while one was open for 9% of the time, Pallas kernels for 12%

profile of v2, /device:TPU:1, one launch (start us, length us, event | category | flops | bytes accessed | tf_op | source)
XLA Modules:
  0.0 152.1 jit_solution(5252077071070323978)
XLA Ops:
  0.7 1.0 slice_bitcast_fusion
  1.7 0.8 slice_bitcast_fusion.2
  2.5 4.6 %collective-permute-start = (bf16[48,1536]{1,0:T(8,128)(2,1)S(1)}, bf16[48,1536]{1,0:T(8,128)(2,1)S(1)}, u32[]{:S(2)}, u32[]{:S(2)}) collective-permute-start(bf16[48,1536]{1,0:T(8,128)(2,1)S(1)} %pad_maximum_fusion.1), channel_id=1, source_target_pairs={{0,8},{8,16},{16,24},{24,32},{32,40},{40,48},{48,56},{56,64},{64,7... | collective-permute-start | bytes 442376 | tf_op jit(solution)/shard_map/ppermute | solution.py:27
  7.1 1.9 %collective-permute-start.1 = (bf16[48,1536]{1,0:T(8,128)(2,1)S(1)}, bf16[48,1536]{1,0:T(8,128)(2,1)S(1)}, u32[]{:S(2)}, u32[]{:S(2)}) collective-permute-start(bf16[48,1536]{1,0:T(8,128)(2,1)S(1)} %pad_maximum_fusion.2), channel_id=1, source_target_pairs={{8,0},{16,8},{24,16},{32,24},{40,32},{48,40},{56,48},{64,56},{72,6... | collective-permute-start | bytes 442376 | tf_op jit(solution)/shard_map/ppermute | solution.py:27
  9.1 0.7 copy.16
  10.3 3.3 %collective-permute-done.1.high_ref = bf16[48,1536]{1,0:T(8,128)(2,1)S(1)} collective-permute-done((bf16[48,1536]{1,0:T(8,128)(2,1)S(1)}, bf16[48,1536]{1,0:T(8,128)(2,1)S(1)}, u32[]{:S(2)}, u32[]{:S(2)}) %collective-permute-start.1) | collective-permute-done | bytes 147488 | tf_op jit(solution)/shard_map/ppermute | solution.py:27
  13.7 8.2 %shard_map.118 = (f32[224,1536]{1,0:T(8,128)S(1)}, f32[2,1536]{1,0:T(2,128)S(1)}, f32[16,2,1536]{2,1,0:T(2,128)}) custom-call(bf16[48,1536]{1,0:T(8,128)(2,1)S(1)} %collective-permute-done.low_ref, bf16[192,1536]{1,0:T(8,128)(2,1)S(1)} %bitcast.30, bf16[48,1536]{1,0:T(8,128)(2,1)S(1)} %collective-permute-done.1.high_ref, ...), custom_call_target="tpu_custom_call" | custom-call | flops 37748736 | bytes 5505024 | tf_op jit(solution)/shard_map/pallas_call | solution.py:297
  21.9 8.0 %all-to-all-start = ((f32[16,2,1536]{2,1,0:T(2,128)}), f32[16,2,1536]{2,1,0:T(2,128)S(1)}, u32[]{:S(2)}, u32[]{:S(2)}) async-start(f32[16,2,1536]{2,1,0:T(2,128)} %get-tuple-element.38), calls=%async_computation | async-start | bytes 393216 | tf_op jit(solution)/shard_map/all_to_all | solution.py:48
  30.0 5.1 %fusion.6.back_ref = f32[224,1536]{1,0:T(8,128)} fusion(bf16[1536,1536]{1,0:T(8,128)(2,1)} %param.12, bf16[16,1536]{1,0:T(8,128)(2,1)S(1)} %slice.77, bf16[192,1536]{1,0:T(8,128)(2,1)} %bitcast.7.own_grad_ref, bf16[16,1536]{1,0:T(8,128)(2,1)S(1)} %slice.76), kind=kOutput, calls=%fused_computation.7 | convolution fusion | flops 1059028992 | bytes 6782976 | tf_op jit(solution)/shard_map/dot_general | solution.py:342
  35.2 1.8 %all-to-all-done = f32[16,2,1536]{2,1,0:T(2,128)S(1)} async-done(((f32[16,2,1536]{2,1,0:T(2,128)}), f32[16,2,1536]{2,1,0:T(2,128)S(1)}, u32[]{:S(2)}, u32[]{:S(2)}) %all-to-all-start) | async-done | bytes 196640 | tf_op jit(solution)/shard_map/all_to_all | solution.py:48
  37.3 0.7 broadcast_in_dim.14
  38.0 8.6 %all-to-all-start.1 = ((f32[16,2,1536]{2,1,0:T(2,128)}), f32[16,2,1536]{2,1,0:T(2,128)S(1)}, u32[]{:S(2)}, u32[]{:S(2)}) async-start(f32[16,2,1536]{2,1,0:T(2,128)} %broadcast_in_dim.14), calls=%async_computation.1 | async-start | bytes 393216 | tf_op jit(solution)/shard_map/all_to_all | solution.py:48
  46.8 7.3 %shard_map.119.product_ref = f32[32,1536]{1,0:T(8,128)S(1)} custom-call(bf16[48,1536]{1,0:T(8,128)(2,1)S(1)} %collective-permute-done.low_ref, bf16[192,1536]{1,0:T(8,128)(2,1)S(1)} %bitcast.32, bf16[48,1536]{1,0:T(8,128)(2,1)S(1)} %collective-permute-done.1.high_ref, s32[256,128]{1,0:T(8,128)S(1)} %broadcast_in_dim.13.ids_ref, ...), custom_call_target="tpu_custom_call" | custom-call | flops 37748736 | bytes 5505024 | tf_op jit(solution)/shard_map/pallas_call | solution.py:297
  54.1 0.8 all-to-all-done.1.all_ref
  54.9 1.3 copy-done.7
  56.2 9.4 %shard_map.120 = (bf16[192,1536]{1,0:T(8,128)(2,1)}, f32[224,1536]{1,0:T(8,128)S(1)}, f32[16,4,1536]{2,1,0:T(4,128)S(1)}, f32[16,4,1536]{2,1,0:T(4,128)S(1)}, f32[2,1536]{1,0:T(2,128)S(1)}) custom-call(s32[1]{0:T(128)} %bitcast.core_ref._, bf16[48,1536]{1,0:T(8,128)(2,1)S(1)} %collective-permute-done.low_ref, bf16[192,1536]{1,0:T(8,128)(2,1)S(1)} %bitcast.33, ...), custom_call_target="tpu_custom_call" | custom-call | flops 37748736 | bytes 5505024 | tf_op jit(solution)/shard_map/pallas_call | solution.py:297
  65.6 1.1 copy-done.5
  66.7 1.0 collective-permute-start.2
  67.7 1.9 %collective-permute-done.2 = f32[16,4,1536]{2,1,0:T(4,128)S(1)} collective-permute-done((f32[16,4,1536]{2,1,0:T(4,128)S(1)}, f32[16,4,1536]{2,1,0:T(4,128)S(1)}, u32[]{:S(2)}, u32[]{:S(2)}) %collective-permute-start.2) | collective-permute-done | bytes 393248 | tf_op jit(solution)/shard_map/ppermute | solution.py:32
  69.5 0.8 add.81
  70.8 5.0 %all-to-all-start.2 = ((f32[16,4,1536]{2,1,0:T(4,128)}), f32[16,4,1536]{2,1,0:T(4,128)}, u32[]{:S(2)}, u32[]{:S(2)}) async-start(f32[16,4,1536]{2,1,0:T(4,128)} %add.81), calls=%async_computation.2 | async-start | bytes 786432 | tf_op jit(solution)/shard_map/all_to_all | solution.py:48
  75.8 3.6 %shard_map.121 = (bf16[16,96,512]{2,1,0:T(8,128)(2,1)S(1)}, bf16[16,112,256]{2,1,0:T(8,128)(2,1)S(1)}) custom-call(s32[1]{0:T(128)} %bitcast.core_ref._, bf16[192,1536]{1,0:T(8,128)(2,1)} %get-tuple-element.52.own_ref, bf16[192,1536]{1,0:T(8,128)(2,1)S(1)} %collective-permute-done.3.other_ref, bf16[192,1536]{1,0:T(8,128)(2,1)} %bitcast.7.own_grad_ref, ...), custom_call_target="tpu_custom_call" | custom-call | flops 905969664 | bytes 7077888 | tf_op jit(solution)/shard_map/pallas_call | solution.py:373
  79.4 0.9 copy-done.1
  80.3 1.1 copy-done.4
  81.4 3.7 %all-to-all-done.2 = f32[16,4,1536]{2,1,0:T(4,128)} async-done(((f32[16,4,1536]{2,1,0:T(4,128)}), f32[16,4,1536]{2,1,0:T(4,128)}, u32[]{:S(2)}, u32[]{:S(2)}) %all-to-all-start.2) | async-done | bytes 393248 | tf_op jit(solution)/shard_map/all_to_all | solution.py:48
  85.1 3.7 %all-to-all-start.3 = ((bf16[16,96,512]{2,1,0:T(8,128)(2,1)}), bf16[16,96,512]{2,1,0:T(8,128)(2,1)S(1)}, u32[]{:S(2)}, u32[]{:S(2)}) async-start(bf16[16,96,512]{2,1,0:T(8,128)(2,1)} %copy-done.4), calls=%async_computation.3 | async-start | bytes 3145728 | tf_op jit(solution)/shard_map/all_to_all | solution.py:48
  88.8 1.1 reduce_sum.58
  89.9 2.2 %collective-permute-start.5 = (f32[4,1536]{1,0:T(4,128)S(1)}, f32[4,1536]{1,0:T(4,128)S(1)}, u32[]{:S(2)}, u32[]{:S(2)}) collective-permute-start(f32[4,1536]{1,0:T(4,128)S(1)} %reduce_sum.58), channel_id=1, source_target_pairs={{0,1},{1,0},{2,3},{3,2},{4,5},{5,4},{6,7},{7,6},{8,9},{9,8},{10,11... | collective-permute-start | bytes 73736 | tf_op jit(solution)/shard_map/ppermute | solution.py:37
  92.0 1.2 collective-permute-done.5
  93.3 1.6 %collective-permute-start.6 = (f32[4,1536]{1,0:T(4,128)S(1)}, f32[4,1536]{1,0:T(4,128)S(1)}, u32[]{:S(2)}, u32[]{:S(2)}) collective-permute-start(f32[4,1536]{1,0:T(4,128)S(1)} %add.82), channel_id=1, source_target_pairs={{0,2},{1,3},{2,0},{3,1},{4,6},{5,7},{6,4},{7,5},{8,10},{9,11},{10,... | collective-permute-start | bytes 73736 | tf_op jit(solution)/shard_map/ppermute | solution.py:37
  94.8 2.4 %collective-permute-done.6 = f32[4,1536]{1,0:T(4,128)S(1)} collective-permute-done((f32[4,1536]{1,0:T(4,128)S(1)}, f32[4,1536]{1,0:T(4,128)S(1)}, u32[]{:S(2)}, u32[]{:S(2)}) %collective-permute-start.6) | collective-permute-done | bytes 24608 | tf_op jit(solution)/shard_map/ppermute | solution.py:37
  97.2 3.1 %collective-permute-start.7 = (f32[4,1536]{1,0:T(4,128)S(1)}, f32[4,1536]{1,0:T(4,128)S(1)}, u32[]{:S(2)}, u32[]{:S(2)}) collective-permute-start(f32[4,1536]{1,0:T(4,128)S(1)} %add.83), channel_id=1, source_target_pairs={{0,4},{1,5},{2,6},{3,7},{4,0},{5,1},{6,2},{7,3},{8,12},{9,13},{10,... | collective-permute-start | bytes 73736 | tf_op jit(solution)/shard_map/ppermute | solution.py:37
  100.3 3.6 %collective-permute-done.7 = f32[4,1536]{1,0:T(4,128)S(1)} collective-permute-done((f32[4,1536]{1,0:T(4,128)S(1)}, f32[4,1536]{1,0:T(4,128)S(1)}, u32[]{:S(2)}, u32[]{:S(2)}) %collective-permute-start.7) | collective-permute-done | bytes 24608 | tf_op jit(solution)/shard_map/ppermute | solution.py:37
  103.9 4.6 %collective-permute-start.8 = (f32[1,1536]{1,0:T(1,128)S(1)}, f32[1,1536]{1,0:T(1,128)S(1)}, u32[]{:S(2)}, u32[]{:S(2)}) collective-permute-start(f32[1,1536]{1,0:T(1,128)S(1)} %slice.80), channel_id=1, source_target_pairs={{0,8},{8,0},{1,9},{9,1},{2,10},{10,2},{3,11},{11,3},{4,12},{12,4},... | collective-permute-start | bytes 18440 | tf_op jit(solution)/shard_map/ppermute | solution.py:37
  108.6 0.8 collective-permute-done.8
  109.5 1.2 copy-done.2
  110.7 0.9 copy-done.3
  111.6 7.0 %all-to-all-start.4 = ((bf16[16,112,256]{2,1,0:T(8,128)(2,1)}), bf16[16,112,256]{2,1,0:T(8,128)(2,1)}, u32[]{:S(2)}, u32[]{:S(2)}) async-start(bf16[16,112,256]{2,1,0:T(8,128)(2,1)} %copy-done.3), calls=%async_computation.4 | async-start | bytes 1835008 | tf_op jit(solution)/shard_map/all_to_all | solution.py:48
  118.6 4.5 %convolution_convert_fusion = bf16[192,1536]{1,0:T(8,128)(2,1)} fusion(bf16[192,1536]{1,0:T(8,128)(2,1)} %get-tuple-element.52.own_ref, bf16[1536,1536]{1,0:T(8,128)(2,1)} %param.12), kind=kOutput, calls=%fused_computation | convolution fusion | flops 906264576 | bytes 5898240 | tf_op jit(solution)/shard_map/dot_general | solution.py:394
  123.1 7.2 %shard_map.123 = bf16[192,1536]{1,0:T(8,128)(2,1)} custom-call(s32[256,128]{1,0:T(8,128)S(1)} %broadcast_in_dim.13.ids_ref, f32[224,1536]{1,0:T(8,128)S(1)} %get-tuple-element.41.conv_ref, f32[224,1536]{1,0:T(8,128)S(1)} %copy-done.6, f32[2,1536]{1,0:T(2,128)S(1)} %get-tuple-element.61.norm_ref, f32[2,1536]{1,0:T(2,128)S(1)} %pad_maximum_fusion.6.sums_ref, ...), custom_call_target="tpu_custom_call" | custom-call | flops 37748736 | bytes 5505024 | tf_op jit(solution)/shard_map/pallas_call | solution.py:297
  130.3 2.3 %all-to-all-done.4.right_ref = bf16[16,112,256]{2,1,0:T(8,128)(2,1)} async-done(((bf16[16,112,256]{2,1,0:T(8,128)(2,1)}), bf16[16,112,256]{2,1,0:T(8,128)(2,1)}, u32[]{:S(2)}, u32[]{:S(2)}) %all-to-all-start.4) | async-done | bytes 917536 | tf_op jit(solution)/shard_map/all_to_all | solution.py:48
  132.6 2.2 %shard_map.124 = (bf16[16,6,768]{2,1,0:T(8,128)(2,1)}, f32[16,1536]{1,0:T(8,128)S(1)}) custom-call(bf16[16,96,512]{2,1,0:T(8,128)(2,1)S(1)} %all-to-all-done.3.left_ref, bf16[16,112,256]{2,1,0:T(8,128)(2,1)} %all-to-all-done.4.right_ref), custom_call_target="tpu_custom_call" | custom-call | tf_op jit(solution)/shard_map/pallas_call | solution.py:422
  134.8 2.8 %collective-permute-start.9 = (f32[16,1536]{1,0:T(8,128)S(1)}, f32[16,1536]{1,0:T(8,128)S(1)}, u32[]{:S(2)}, u32[]{:S(2)}) collective-permute-start(f32[16,1536]{1,0:T(8,128)S(1)} %get-tuple-element.68), channel_id=1, source_target_pairs={{0,8},{8,0},{1,9},{9,1},{2,10},{10,2},{3,11},{11,3},{4,12},{12,4},... | collective-permute-start | bytes 294920 | tf_op jit(solution)/shard_map/ppermute | solution.py:37
  137.6 0.6 slice_reduce_fusion.1
  138.2 4.9 %all-to-all-start.5 = ((bf16[16,6,768]{2,1,0:T(8,128)(2,1)}), bf16[16,6,768]{2,1,0:T(8,128)(2,1)S(1)}, u32[]{:S(2)}, u32[]{:S(2)}) async-start(bf16[16,6,768]{2,1,0:T(8,128)(2,1)} %get-tuple-element.69), calls=%async_computation.5 | async-start | bytes 393216 | tf_op jit(solution)/shard_map/all_to_all | solution.py:48
  143.2 0.7 pad_maximum_fusion
  143.9 7.6 %all-to-all-done.5 = bf16[16,6,768]{2,1,0:T(8,128)(2,1)S(1)} async-done(((bf16[16,6,768]{2,1,0:T(8,128)(2,1)}), bf16[16,6,768]{2,1,0:T(8,128)(2,1)S(1)}, u32[]{:S(2)}, u32[]{:S(2)}) %all-to-all-start.5) | async-done | bytes 147488 | tf_op jit(solution)/shard_map/all_to_all | solution.py:48
  151.5 0.6 pad_maximum_fusion.3
  (60 shorter events, 1.7 us)
Async XLA Ops:
  0.6 13.1 %copy-start = (bf16[1,192,1536]{2,1,0:T(8,128)(2,1)S(1)}, bf16[1,192,1536]{2,1,0:T(8,128)(2,1)}, u32[]{:S(2)}) copy-start(bf16[1,192,1536]{2,1,0:T(8,128)(2,1)} %param.8) | copy-start | bytes 1769476
  0.6 13.1 %copy-start.8 = (f32[32,1536]{1,0:T(8,128)S(1)}, f32[32,1536]{1,0:T(8,128)}, u32[]{:S(2)}) copy-start(f32[32,1536]{1,0:T(8,128)} %taps_ref.3) | copy-start | bytes 589828
  2.5 7.8 %collective-permute-start = (bf16[48,1536]{1,0:T(8,128)(2,1)S(1)}, bf16[48,1536]{1,0:T(8,128)(2,1)S(1)}, u32[]{:S(2)}, u32[]{:S(2)}) collective-permute-start(bf16[48,1536]{1,0:T(8,128)(2,1)S(1)} %pad_maximum_fusion.1), channel_id=1, source_target_pairs={{0,8},{8,16},{16,24},{24,32},{32,40},{40,48},{48,56},{56,64},{64,7... | collective-permute-start | bytes 442376 | tf_op jit(solution)/shard_map/ppermute | solution.py:27
  7.1 6.5 %collective-permute-start.1 = (bf16[48,1536]{1,0:T(8,128)(2,1)S(1)}, bf16[48,1536]{1,0:T(8,128)(2,1)S(1)}, u32[]{:S(2)}, u32[]{:S(2)}) collective-permute-start(bf16[48,1536]{1,0:T(8,128)(2,1)S(1)} %pad_maximum_fusion.2), channel_id=1, source_target_pairs={{8,0},{16,8},{24,16},{32,24},{40,32},{48,40},{56,48},{64,56},{72,6... | collective-permute-start | bytes 442376 | tf_op jit(solution)/shard_map/ppermute | solution.py:27
  21.9 15.0 %all-to-all-start = ((f32[16,2,1536]{2,1,0:T(2,128)}), f32[16,2,1536]{2,1,0:T(2,128)S(1)}, u32[]{:S(2)}, u32[]{:S(2)}) async-start(f32[16,2,1536]{2,1,0:T(2,128)} %get-tuple-element.38), calls=%async_computation | async-start | bytes 393216 | tf_op jit(solution)/shard_map/all_to_all | solution.py:48
  29.9 5.2 %copy-start.9 = (f32[1536]{0:T(1024)S(1)}, f32[1536]{0:T(1024)}, u32[]{:S(2)}) copy-start(f32[1536]{0:T(1024)} %param.10) | copy-start | bytes 18436
  30.0 5.2 %copy-start.10 = (f32[1536]{0:T(1024)S(1)}, f32[1536]{0:T(1024)}, u32[]{:S(2)}) copy-start(f32[1536]{0:T(1024)} %param.11) | copy-start | bytes 18436
  38.0 16.9 %all-to-all-start.1 = ((f32[16,2,1536]{2,1,0:T(2,128)}), f32[16,2,1536]{2,1,0:T(2,128)S(1)}, u32[]{:S(2)}, u32[]{:S(2)}) async-start(f32[16,2,1536]{2,1,0:T(2,128)} %broadcast_in_dim.14), calls=%async_computation.1 | async-start | bytes 393216 | tf_op jit(solution)/shard_map/all_to_all | solution.py:48
  54.9 1.3 copy-start.7
  65.6 1.1 copy-start.5
  66.7 2.9 %collective-permute-start.2 = (f32[16,4,1536]{2,1,0:T(4,128)S(1)}, f32[16,4,1536]{2,1,0:T(4,128)S(1)}, u32[]{:S(2)}, u32[]{:S(2)}) collective-permute-start(f32[16,4,1536]{2,1,0:T(4,128)S(1)} %get-tuple-element.49), channel_id=1, source_target_pairs={{0,8},{8,0},{1,9},{9,1},{2,10},{10,2},{3,11},{11,3},{4,12},{12,4},... | collective-permute-start | bytes 1179656 | tf_op jit(solution)/shard_map/ppermute | solution.py:32
  67.7 8.1 %collective-permute-start.4 = (bf16[192,1536]{1,0:T(8,128)(2,1)}, bf16[192,1536]{1,0:T(8,128)(2,1)S(1)}, u32[]{:S(2)}, u32[]{:S(2)}) collective-permute-start(bf16[192,1536]{1,0:T(8,128)(2,1)} %bitcast.7.own_grad_ref), channel_id=1, source_target_pairs={{0,8},{8,0},{1,9},{9,1},{2,10},{10,2},{3,11},{11,3},{4,12},{12,4},... | collective-permute-start | bytes 1769480 | tf_op jit(solution)/shard_map/ppermute | solution.py:32
  70.4 5.4 %collective-permute-start.3 = (bf16[192,1536]{1,0:T(8,128)(2,1)}, bf16[192,1536]{1,0:T(8,128)(2,1)S(1)}, u32[]{:S(2)}, u32[]{:S(2)}) collective-permute-start(bf16[192,1536]{1,0:T(8,128)(2,1)} %get-tuple-element.52.own_ref), channel_id=1, source_target_pairs={{0,8},{8,0},{1,9},{9,1},{2,10},{10,2},{3,11},{11,3},{4,12},{12,4},... | collective-permute-start | bytes 1769480 | tf_op jit(solution)/shard_map/ppermute | solution.py:32
  70.8 14.3 %all-to-all-start.2 = ((f32[16,4,1536]{2,1,0:T(4,128)}), f32[16,4,1536]{2,1,0:T(4,128)}, u32[]{:S(2)}, u32[]{:S(2)}) async-start(f32[16,4,1536]{2,1,0:T(4,128)} %add.81), calls=%async_computation.2 | async-start | bytes 786432 | tf_op jit(solution)/shard_map/all_to_all | solution.py:48
  79.3 0.9 copy-start.1
  80.3 1.2 copy-start.4
  85.1 24.4 %all-to-all-start.3 = ((bf16[16,96,512]{2,1,0:T(8,128)(2,1)}), bf16[16,96,512]{2,1,0:T(8,128)(2,1)S(1)}, u32[]{:S(2)}, u32[]{:S(2)}) async-start(bf16[16,96,512]{2,1,0:T(8,128)(2,1)} %copy-done.4), calls=%async_computation.3 | async-start | bytes 3145728 | tf_op jit(solution)/shard_map/all_to_all | solution.py:48
  89.9 3.4 %collective-permute-start.5 = (f32[4,1536]{1,0:T(4,128)S(1)}, f32[4,1536]{1,0:T(4,128)S(1)}, u32[]{:S(2)}, u32[]{:S(2)}) collective-permute-start(f32[4,1536]{1,0:T(4,128)S(1)} %reduce_sum.58), channel_id=1, source_target_pairs={{0,1},{1,0},{2,3},{3,2},{4,5},{5,4},{6,7},{7,6},{8,9},{9,8},{10,11... | collective-permute-start | bytes 73736 | tf_op jit(solution)/shard_map/ppermute | solution.py:37
  93.3 4.0 %collective-permute-start.6 = (f32[4,1536]{1,0:T(4,128)S(1)}, f32[4,1536]{1,0:T(4,128)S(1)}, u32[]{:S(2)}, u32[]{:S(2)}) collective-permute-start(f32[4,1536]{1,0:T(4,128)S(1)} %add.82), channel_id=1, source_target_pairs={{0,2},{1,3},{2,0},{3,1},{4,6},{5,7},{6,4},{7,5},{8,10},{9,11},{10,... | collective-permute-start | bytes 73736 | tf_op jit(solution)/shard_map/ppermute | solution.py:37
  97.2 6.7 %collective-permute-start.7 = (f32[4,1536]{1,0:T(4,128)S(1)}, f32[4,1536]{1,0:T(4,128)S(1)}, u32[]{:S(2)}, u32[]{:S(2)}) collective-permute-start(f32[4,1536]{1,0:T(4,128)S(1)} %add.83), channel_id=1, source_target_pairs={{0,4},{1,5},{2,6},{3,7},{4,0},{5,1},{6,2},{7,3},{8,12},{9,13},{10,... | collective-permute-start | bytes 73736 | tf_op jit(solution)/shard_map/ppermute | solution.py:37
  103.9 5.5 %collective-permute-start.8 = (f32[1,1536]{1,0:T(1,128)S(1)}, f32[1,1536]{1,0:T(1,128)S(1)}, u32[]{:S(2)}, u32[]{:S(2)}) collective-permute-start(f32[1,1536]{1,0:T(1,128)S(1)} %slice.80), channel_id=1, source_target_pairs={{0,8},{8,0},{1,9},{9,1},{2,10},{10,2},{3,11},{11,3},{4,12},{12,4},... | collective-permute-start | bytes 18440 | tf_op jit(solution)/shard_map/ppermute | solution.py:37
  109.4 1.2 copy-start.2
  110.7 0.9 copy-start.3
  111.6 21.0 %all-to-all-start.4 = ((bf16[16,112,256]{2,1,0:T(8,128)(2,1)}), bf16[16,112,256]{2,1,0:T(8,128)(2,1)}, u32[]{:S(2)}, u32[]{:S(2)}) async-start(bf16[16,112,256]{2,1,0:T(8,128)(2,1)} %copy-done.3), calls=%async_computation.4 | async-start | bytes 1835008 | tf_op jit(solution)/shard_map/all_to_all | solution.py:48
  118.6 4.5 %copy-start.6 = (f32[224,1536]{1,0:T(8,128)S(1)}, f32[224,1536]{1,0:T(8,128)}, u32[]{:S(2)}) copy-start(f32[224,1536]{1,0:T(8,128)} %copy-done.5) | copy-start | bytes 4128772
  134.8 8.4 %collective-permute-start.9 = (f32[16,1536]{1,0:T(8,128)S(1)}, f32[16,1536]{1,0:T(8,128)S(1)}, u32[]{:S(2)}, u32[]{:S(2)}) collective-permute-start(f32[16,1536]{1,0:T(8,128)S(1)} %get-tuple-element.68), channel_id=1, source_target_pairs={{0,8},{8,0},{1,9},{9,1},{2,10},{10,2},{3,11},{11,3},{4,12},{12,4},... | collective-permute-start | bytes 294920 | tf_op jit(solution)/shard_map/ppermute | solution.py:37
  138.2 13.2 %all-to-all-start.5 = ((bf16[16,6,768]{2,1,0:T(8,128)(2,1)}), bf16[16,6,768]{2,1,0:T(8,128)(2,1)S(1)}, u32[]{:S(2)}, u32[]{:S(2)}) async-start(bf16[16,6,768]{2,1,0:T(8,128)(2,1)} %get-tuple-element.69), calls=%async_computation.5 | async-start | bytes 393216 | tf_op jit(solution)/shard_map/all_to_all | solution.py:48

commit v3 on v1

--- a/solution.py
+++ b/solution.py
@@ -274,7 +274,7 @@
     out_ref[...] = result[...].astype(jnp.bfloat16)
 
 
-PARAMS = pltpu.CompilerParams(vmem_limit_bytes=16 * 1024 * 1024)
+PARAMS = pltpu.CompilerParams(vmem_limit_bytes=12 * 1024 * 1024)
 
 
 def cut(shape, width):

time: 153 us -> 153 us (level)
  no operation moved by 1% of the time
where the time goes in v3:
time: 153 us; the launch traced here: 152 us
  starting transfers between devices  59.2 us (39%)
  Pallas kernels  38.2 us (25%)
  waiting for transfers between devices  29.1 us (19%)
  local copies, waits for them, and re-layouts  10.7 us (7%)
  matrix products  9.89 us (6%)
  other arithmetic  4.06 us (3%)
    all_to_all x6, starting transfers between devices, exchanged(): return lax.all_to_all(blocks, axes, 0, 0, tiled=True)  37.2 us
    pallas_call x4, Pallas kernels, call(): pl.pallas_call(kernel, grid=(width // TILE,), in_specs=[cut(a.shape, widt...  32.3 us
    all_to_all x6, waiting for transfers between devices, exchanged(): return lax.all_to_all(blocks, axes, 0, 0, tiled=True)  16 us
    ppermute x5, starting transfers between devices, crossed(): return lax.ppermute(value, axis, [(i, i ^ bit) for i in range(count)])  14.1 us
    ppermute x5, waiting for transfers between devices, crossed(): return lax.ppermute(value, axis, [(i, i ^ bit) for i in range(count)])  7.92 us
    unnamed x22, local copies, waits for them, and re-layouts  6.6 us
    ppermute x2, starting transfers between devices, shifted(): return lax.ppermute(value, axes, pairs)  6.52 us
    dot_general x1, matrix products, local(): lax.dot_general(grads_wide, proj_weight, (((1,), (1,)), ((), ())), prefer...  5.16 us
  transfers between devices with their start and end apart: 16, of which 12 were waited for; matrix products, arithmetic and copies ran while one was open for 9% of the time, Pallas kernels for 12%

profile of v3, /device:TPU:1, one launch (start us, length us, event | category | flops | bytes accessed | tf_op | source)
XLA Modules:
  0.0 152.1 jit_solution(2409408029197780204)
XLA Ops:
  0.7 1.0 slice_bitcast_fusion
  1.7 0.8 slice_bitcast_fusion.2
  2.5 4.6 %collective-permute-start = (bf16[48,1536]{1,0:T(8,128)(2,1)S(1)}, bf16[48,1536]{1,0:T(8,128)(2,1)S(1)}, u32[]{:S(2)}, u32[]{:S(2)}) collective-permute-start(bf16[48,1536]{1,0:T(8,128)(2,1)S(1)} %pad_maximum_fusion.1), channel_id=1, source_target_pairs={{0,8},{8,16},{16,24},{24,32},{32,40},{40,48},{48,56},{56,64},{64,7... | collective-permute-start | bytes 442376 | tf_op jit(solution)/shard_map/ppermute | solution.py:27
  7.1 1.9 %collective-permute-start.1 = (bf16[48,1536]{1,0:T(8,128)(2,1)S(1)}, bf16[48,1536]{1,0:T(8,128)(2,1)S(1)}, u32[]{:S(2)}, u32[]{:S(2)}) collective-permute-start(bf16[48,1536]{1,0:T(8,128)(2,1)S(1)} %pad_maximum_fusion.2), channel_id=1, source_target_pairs={{8,0},{16,8},{24,16},{32,24},{40,32},{48,40},{56,48},{64,56},{72,6... | collective-permute-start | bytes 442376 | tf_op jit(solution)/shard_map/ppermute | solution.py:27
  9.1 0.7 copy.16
  10.3 3.3 %collective-permute-done.1.high_ref = bf16[48,1536]{1,0:T(8,128)(2,1)S(1)} collective-permute-done((bf16[48,1536]{1,0:T(8,128)(2,1)S(1)}, bf16[48,1536]{1,0:T(8,128)(2,1)S(1)}, u32[]{:S(2)}, u32[]{:S(2)}) %collective-permute-start.1) | collective-permute-done | bytes 147488 | tf_op jit(solution)/shard_map/ppermute | solution.py:27
  13.7 8.3 %shard_map.118 = (f32[224,1536]{1,0:T(8,128)S(1)}, f32[2,1536]{1,0:T(2,128)S(1)}, f32[16,2,1536]{2,1,0:T(2,128)}) custom-call(bf16[48,1536]{1,0:T(8,128)(2,1)S(1)} %collective-permute-done.low_ref, bf16[192,1536]{1,0:T(8,128)(2,1)S(1)} %bitcast.30, bf16[48,1536]{1,0:T(8,128)(2,1)S(1)} %collective-permute-done.1.high_ref, ...), custom_call_target="tpu_custom_call" | custom-call | flops 37748736 | bytes 5505024 | tf_op jit(solution)/shard_map/pallas_call | solution.py:290
  22.0 8.0 %all-to-all-start = ((f32[16,2,1536]{2,1,0:T(2,128)}), f32[16,2,1536]{2,1,0:T(2,128)S(1)}, u32[]{:S(2)}, u32[]{:S(2)}) async-start(f32[16,2,1536]{2,1,0:T(2,128)} %get-tuple-element.38), calls=%async_computation | async-start | bytes 393216 | tf_op jit(solution)/shard_map/all_to_all | solution.py:48
  30.0 5.2 %fusion.6.back_ref = f32[224,1536]{1,0:T(8,128)} fusion(bf16[1536,1536]{1,0:T(8,128)(2,1)} %param.12, bf16[16,1536]{1,0:T(8,128)(2,1)S(1)} %slice.77, bf16[192,1536]{1,0:T(8,128)(2,1)} %bitcast.7.own_grad_ref, bf16[16,1536]{1,0:T(8,128)(2,1)S(1)} %slice.76), kind=kOutput, calls=%fused_computation.7 | convolution fusion | flops 1059028992 | bytes 6782976 | tf_op jit(solution)/shard_map/dot_general | solution.py:335
  35.2 1.7 %all-to-all-done = f32[16,2,1536]{2,1,0:T(2,128)S(1)} async-done(((f32[16,2,1536]{2,1,0:T(2,128)}), f32[16,2,1536]{2,1,0:T(2,128)S(1)}, u32[]{:S(2)}, u32[]{:S(2)}) %all-to-all-start) | async-done | bytes 196640 | tf_op jit(solution)/shard_map/all_to_all | solution.py:48
  37.3 0.7 broadcast_in_dim.14
  38.0 8.6 %all-to-all-start.1 = ((f32[16,2,1536]{2,1,0:T(2,128)}), f32[16,2,1536]{2,1,0:T(2,128)S(1)}, u32[]{:S(2)}, u32[]{:S(2)}) async-start(f32[16,2,1536]{2,1,0:T(2,128)} %broadcast_in_dim.14), calls=%async_computation.1 | async-start | bytes 393216 | tf_op jit(solution)/shard_map/all_to_all | solution.py:48
  46.9 7.3 %shard_map.119.product_ref = f32[32,1536]{1,0:T(8,128)S(1)} custom-call(bf16[48,1536]{1,0:T(8,128)(2,1)S(1)} %collective-permute-done.low_ref, bf16[192,1536]{1,0:T(8,128)(2,1)S(1)} %bitcast.32, bf16[48,1536]{1,0:T(8,128)(2,1)S(1)} %collective-permute-done.1.high_ref, s32[256,128]{1,0:T(8,128)S(1)} %broadcast_in_dim.13.ids_ref, ...), custom_call_target="tpu_custom_call" | custom-call | flops 37748736 | bytes 5505024 | tf_op jit(solution)/shard_map/pallas_call | solution.py:290
  54.2 0.7 all-to-all-done.1.all_ref
  54.9 1.3 copy-done.7
  56.3 9.5 %shard_map.120 = (bf16[192,1536]{1,0:T(8,128)(2,1)}, f32[224,1536]{1,0:T(8,128)S(1)}, f32[16,4,1536]{2,1,0:T(4,128)S(1)}, f32[16,4,1536]{2,1,0:T(4,128)S(1)}, f32[2,1536]{1,0:T(2,128)S(1)}) custom-call(s32[1]{0:T(128)} %bitcast.core_ref._, bf16[48,1536]{1,0:T(8,128)(2,1)S(1)} %collective-permute-done.low_ref, bf16[192,1536]{1,0:T(8,128)(2,1)S(1)} %bitcast.33, ...), custom_call_target="tpu_custom_call" | custom-call | flops 37748736 | bytes 5505024 | tf_op jit(solution)/shard_map/pallas_call | solution.py:290
  65.8 1.1 copy-done.5
  66.9 1.0 collective-permute-start.2
  67.9 1.9 %collective-permute-done.2 = f32[16,4,1536]{2,1,0:T(4,128)S(1)} collective-permute-done((f32[16,4,1536]{2,1,0:T(4,128)S(1)}, f32[16,4,1536]{2,1,0:T(4,128)S(1)}, u32[]{:S(2)}, u32[]{:S(2)}) %collective-permute-start.2) | collective-permute-done | bytes 393248 | tf_op jit(solution)/shard_map/ppermute | solution.py:32
  69.7 0.8 add.81
  71.0 5.0 %all-to-all-start.2 = ((f32[16,4,1536]{2,1,0:T(4,128)}), f32[16,4,1536]{2,1,0:T(4,128)}, u32[]{:S(2)}, u32[]{:S(2)}) async-start(f32[16,4,1536]{2,1,0:T(4,128)} %add.81), calls=%async_computation.2 | async-start | bytes 786432 | tf_op jit(solution)/shard_map/all_to_all | solution.py:48
  76.0 3.6 %shard_map.121 = (bf16[16,96,512]{2,1,0:T(8,128)(2,1)S(1)}, bf16[16,112,256]{2,1,0:T(8,128)(2,1)S(1)}) custom-call(s32[1]{0:T(128)} %bitcast.core_ref._, bf16[192,1536]{1,0:T(8,128)(2,1)} %get-tuple-element.52.own_ref, bf16[192,1536]{1,0:T(8,128)(2,1)S(1)} %collective-permute-done.3.other_ref, bf16[192,1536]{1,0:T(8,128)(2,1)} %bitcast.7.own_grad_ref, ...), custom_call_target="tpu_custom_call" | custom-call | flops 905969664 | bytes 7077888 | tf_op jit(solution)/shard_map/pallas_call | solution.py:366
  79.6 0.9 copy-done.1
  80.5 1.1 copy-done.4
  81.6 3.7 %all-to-all-done.2 = f32[16,4,1536]{2,1,0:T(4,128)} async-done(((f32[16,4,1536]{2,1,0:T(4,128)}), f32[16,4,1536]{2,1,0:T(4,128)}, u32[]{:S(2)}, u32[]{:S(2)}) %all-to-all-start.2) | async-done | bytes 393248 | tf_op jit(solution)/shard_map/all_to_all | solution.py:48
  85.3 3.7 %all-to-all-start.3 = ((bf16[16,96,512]{2,1,0:T(8,128)(2,1)}), bf16[16,96,512]{2,1,0:T(8,128)(2,1)S(1)}, u32[]{:S(2)}, u32[]{:S(2)}) async-start(bf16[16,96,512]{2,1,0:T(8,128)(2,1)} %copy-done.4), calls=%async_computation.3 | async-start | bytes 3145728 | tf_op jit(solution)/shard_map/all_to_all | solution.py:48
  89.0 1.1 reduce_sum.58
  90.1 2.2 %collective-permute-start.5 = (f32[4,1536]{1,0:T(4,128)S(1)}, f32[4,1536]{1,0:T(4,128)S(1)}, u32[]{:S(2)}, u32[]{:S(2)}) collective-permute-start(f32[4,1536]{1,0:T(4,128)S(1)} %reduce_sum.58), channel_id=1, source_target_pairs={{0,1},{1,0},{2,3},{3,2},{4,5},{5,4},{6,7},{7,6},{8,9},{9,8},{10,11... | collective-permute-start | bytes 73736 | tf_op jit(solution)/shard_map/ppermute | solution.py:37
  92.2 1.2 collective-permute-done.5
  93.5 1.6 %collective-permute-start.6 = (f32[4,1536]{1,0:T(4,128)S(1)}, f32[4,1536]{1,0:T(4,128)S(1)}, u32[]{:S(2)}, u32[]{:S(2)}) collective-permute-start(f32[4,1536]{1,0:T(4,128)S(1)} %add.82), channel_id=1, source_target_pairs={{0,2},{1,3},{2,0},{3,1},{4,6},{5,7},{6,4},{7,5},{8,10},{9,11},{10,... | collective-permute-start | bytes 73736 | tf_op jit(solution)/shard_map/ppermute | solution.py:37
  95.0 2.4 %collective-permute-done.6 = f32[4,1536]{1,0:T(4,128)S(1)} collective-permute-done((f32[4,1536]{1,0:T(4,128)S(1)}, f32[4,1536]{1,0:T(4,128)S(1)}, u32[]{:S(2)}, u32[]{:S(2)}) %collective-permute-start.6) | collective-permute-done | bytes 24608 | tf_op jit(solution)/shard_map/ppermute | solution.py:37
  97.4 3.2 %collective-permute-start.7 = (f32[4,1536]{1,0:T(4,128)S(1)}, f32[4,1536]{1,0:T(4,128)S(1)}, u32[]{:S(2)}, u32[]{:S(2)}) collective-permute-start(f32[4,1536]{1,0:T(4,128)S(1)} %add.83), channel_id=1, source_target_pairs={{0,4},{1,5},{2,6},{3,7},{4,0},{5,1},{6,2},{7,3},{8,12},{9,13},{10,... | collective-permute-start | bytes 73736 | tf_op jit(solution)/shard_map/ppermute | solution.py:37
  100.6 3.5 %collective-permute-done.7 = f32[4,1536]{1,0:T(4,128)S(1)} collective-permute-done((f32[4,1536]{1,0:T(4,128)S(1)}, f32[4,1536]{1,0:T(4,128)S(1)}, u32[]{:S(2)}, u32[]{:S(2)}) %collective-permute-start.7) | collective-permute-done | bytes 24608 | tf_op jit(solution)/shard_map/ppermute | solution.py:37
  104.1 4.5 %collective-permute-start.8 = (f32[1,1536]{1,0:T(1,128)S(1)}, f32[1,1536]{1,0:T(1,128)S(1)}, u32[]{:S(2)}, u32[]{:S(2)}) collective-permute-start(f32[1,1536]{1,0:T(1,128)S(1)} %slice.80), channel_id=1, source_target_pairs={{0,8},{8,0},{1,9},{9,1},{2,10},{10,2},{3,11},{11,3},{4,12},{12,4},... | collective-permute-start | bytes 18440 | tf_op jit(solution)/shard_map/ppermute | solution.py:37
  108.6 0.8 collective-permute-done.8
  109.6 1.2 copy-done.2
  110.8 0.9 copy-done.3
  111.7 6.9 %all-to-all-start.4 = ((bf16[16,112,256]{2,1,0:T(8,128)(2,1)}), bf16[16,112,256]{2,1,0:T(8,128)(2,1)}, u32[]{:S(2)}, u32[]{:S(2)}) async-start(bf16[16,112,256]{2,1,0:T(8,128)(2,1)} %copy-done.3), calls=%async_computation.4 | async-start | bytes 1835008 | tf_op jit(solution)/shard_map/all_to_all | solution.py:48
  118.6 4.5 %convolution_convert_fusion = bf16[192,1536]{1,0:T(8,128)(2,1)} fusion(bf16[192,1536]{1,0:T(8,128)(2,1)} %get-tuple-element.52.own_ref, bf16[1536,1536]{1,0:T(8,128)(2,1)} %param.12), kind=kOutput, calls=%fused_computation | convolution fusion | flops 906264576 | bytes 5898240 | tf_op jit(solution)/shard_map/dot_general | solution.py:387
  123.1 7.2 %shard_map.123 = bf16[192,1536]{1,0:T(8,128)(2,1)} custom-call(s32[256,128]{1,0:T(8,128)S(1)} %broadcast_in_dim.13.ids_ref, f32[224,1536]{1,0:T(8,128)S(1)} %get-tuple-element.41.conv_ref, f32[224,1536]{1,0:T(8,128)S(1)} %copy-done.6, f32[2,1536]{1,0:T(2,128)S(1)} %get-tuple-element.61.norm_ref, f32[2,1536]{1,0:T(2,128)S(1)} %pad_maximum_fusion.6.sums_ref, ...), custom_call_target="tpu_custom_call" | custom-call | flops 37748736 | bytes 5505024 | tf_op jit(solution)/shard_map/pallas_call | solution.py:290
  130.3 2.2 %all-to-all-done.4.right_ref = bf16[16,112,256]{2,1,0:T(8,128)(2,1)} async-done(((bf16[16,112,256]{2,1,0:T(8,128)(2,1)}), bf16[16,112,256]{2,1,0:T(8,128)(2,1)}, u32[]{:S(2)}, u32[]{:S(2)}) %all-to-all-start.4) | async-done | bytes 917536 | tf_op jit(solution)/shard_map/all_to_all | solution.py:48
  132.5 2.2 %shard_map.124 = (bf16[16,6,768]{2,1,0:T(8,128)(2,1)}, f32[16,1536]{1,0:T(8,128)S(1)}) custom-call(bf16[16,96,512]{2,1,0:T(8,128)(2,1)S(1)} %all-to-all-done.3.left_ref, bf16[16,112,256]{2,1,0:T(8,128)(2,1)} %all-to-all-done.4.right_ref), custom_call_target="tpu_custom_call" | custom-call | tf_op jit(solution)/shard_map/pallas_call | solution.py:415
  134.7 2.8 %collective-permute-start.9 = (f32[16,1536]{1,0:T(8,128)S(1)}, f32[16,1536]{1,0:T(8,128)S(1)}, u32[]{:S(2)}, u32[]{:S(2)}) collective-permute-start(f32[16,1536]{1,0:T(8,128)S(1)} %get-tuple-element.68), channel_id=1, source_target_pairs={{0,8},{8,0},{1,9},{9,1},{2,10},{10,2},{3,11},{11,3},{4,12},{12,4},... | collective-permute-start | bytes 294920 | tf_op jit(solution)/shard_map/ppermute | solution.py:37
  137.5 0.6 slice_reduce_fusion.1
  138.1 5.1 %all-to-all-start.5 = ((bf16[16,6,768]{2,1,0:T(8,128)(2,1)}), bf16[16,6,768]{2,1,0:T(8,128)(2,1)S(1)}, u32[]{:S(2)}, u32[]{:S(2)}) async-start(bf16[16,6,768]{2,1,0:T(8,128)(2,1)} %get-tuple-element.69), calls=%async_computation.5 | async-start | bytes 393216 | tf_op jit(solution)/shard_map/all_to_all | solution.py:48
  143.2 0.7 pad_maximum_fusion
  143.9 7.6 %all-to-all-done.5 = bf16[16,6,768]{2,1,0:T(8,128)(2,1)S(1)} async-done(((bf16[16,6,768]{2,1,0:T(8,128)(2,1)}), bf16[16,6,768]{2,1,0:T(8,128)(2,1)S(1)}, u32[]{:S(2)}, u32[]{:S(2)}) %all-to-all-start.5) | async-done | bytes 147488 | tf_op jit(solution)/shard_map/all_to_all | solution.py:48
  151.5 0.6 pad_maximum_fusion.3
  (60 shorter events, 1.8 us)
Async XLA Ops:
  0.6 13.1 %copy-start = (bf16[1,192,1536]{2,1,0:T(8,128)(2,1)S(1)}, bf16[1,192,1536]{2,1,0:T(8,128)(2,1)}, u32[]{:S(2)}) copy-start(bf16[1,192,1536]{2,1,0:T(8,128)(2,1)} %param.8) | copy-start | bytes 1769476
  0.6 13.1 %copy-start.8 = (f32[32,1536]{1,0:T(8,128)S(1)}, f32[32,1536]{1,0:T(8,128)}, u32[]{:S(2)}) copy-start(f32[32,1536]{1,0:T(8,128)} %taps_ref.3) | copy-start | bytes 589828
  2.5 7.8 %collective-permute-start = (bf16[48,1536]{1,0:T(8,128)(2,1)S(1)}, bf16[48,1536]{1,0:T(8,128)(2,1)S(1)}, u32[]{:S(2)}, u32[]{:S(2)}) collective-permute-start(bf16[48,1536]{1,0:T(8,128)(2,1)S(1)} %pad_maximum_fusion.1), channel_id=1, source_target_pairs={{0,8},{8,16},{16,24},{24,32},{32,40},{40,48},{48,56},{56,64},{64,7... | collective-permute-start | bytes 442376 | tf_op jit(solution)/shard_map/ppermute | solution.py:27
  7.1 6.5 %collective-permute-start.1 = (bf16[48,1536]{1,0:T(8,128)(2,1)S(1)}, bf16[48,1536]{1,0:T(8,128)(2,1)S(1)}, u32[]{:S(2)}, u32[]{:S(2)}) collective-permute-start(bf16[48,1536]{1,0:T(8,128)(2,1)S(1)} %pad_maximum_fusion.2), channel_id=1, source_target_pairs={{8,0},{16,8},{24,16},{32,24},{40,32},{48,40},{56,48},{64,56},{72,6... | collective-permute-start | bytes 442376 | tf_op jit(solution)/shard_map/ppermute | solution.py:27
  22.0 15.0 %all-to-all-start = ((f32[16,2,1536]{2,1,0:T(2,128)}), f32[16,2,1536]{2,1,0:T(2,128)S(1)}, u32[]{:S(2)}, u32[]{:S(2)}) async-start(f32[16,2,1536]{2,1,0:T(2,128)} %get-tuple-element.38), calls=%async_computation | async-start | bytes 393216 | tf_op jit(solution)/shard_map/all_to_all | solution.py:48
  30.0 5.2 %copy-start.9 = (f32[1536]{0:T(1024)S(1)}, f32[1536]{0:T(1024)}, u32[]{:S(2)}) copy-start(f32[1536]{0:T(1024)} %param.10) | copy-start | bytes 18436
  30.0 5.2 %copy-start.10 = (f32[1536]{0:T(1024)S(1)}, f32[1536]{0:T(1024)}, u32[]{:S(2)}) copy-start(f32[1536]{0:T(1024)} %param.11) | copy-start | bytes 18436
  38.0 16.9 %all-to-all-start.1 = ((f32[16,2,1536]{2,1,0:T(2,128)}), f32[16,2,1536]{2,1,0:T(2,128)S(1)}, u32[]{:S(2)}, u32[]{:S(2)}) async-start(f32[16,2,1536]{2,1,0:T(2,128)} %broadcast_in_dim.14), calls=%async_computation.1 | async-start | bytes 393216 | tf_op jit(solution)/shard_map/all_to_all | solution.py:48
  54.9 1.3 copy-start.7
  65.8 1.1 copy-start.5
  66.9 2.9 %collective-permute-start.2 = (f32[16,4,1536]{2,1,0:T(4,128)S(1)}, f32[16,4,1536]{2,1,0:T(4,128)S(1)}, u32[]{:S(2)}, u32[]{:S(2)}) collective-permute-start(f32[16,4,1536]{2,1,0:T(4,128)S(1)} %get-tuple-element.49), channel_id=1, source_target_pairs={{0,8},{8,0},{1,9},{9,1},{2,10},{10,2},{3,11},{11,3},{4,12},{12,4},... | collective-permute-start | bytes 1179656 | tf_op jit(solution)/shard_map/ppermute | solution.py:32
  67.9 8.1 %collective-permute-start.4 = (bf16[192,1536]{1,0:T(8,128)(2,1)}, bf16[192,1536]{1,0:T(8,128)(2,1)S(1)}, u32[]{:S(2)}, u32[]{:S(2)}) collective-permute-start(bf16[192,1536]{1,0:T(8,128)(2,1)} %bitcast.7.own_grad_ref), channel_id=1, source_target_pairs={{0,8},{8,0},{1,9},{9,1},{2,10},{10,2},{3,11},{11,3},{4,12},{12,4},... | collective-permute-start | bytes 1769480 | tf_op jit(solution)/shard_map/ppermute | solution.py:32
  70.6 5.4 %collective-permute-start.3 = (bf16[192,1536]{1,0:T(8,128)(2,1)}, bf16[192,1536]{1,0:T(8,128)(2,1)S(1)}, u32[]{:S(2)}, u32[]{:S(2)}) collective-permute-start(bf16[192,1536]{1,0:T(8,128)(2,1)} %get-tuple-element.52.own_ref), channel_id=1, source_target_pairs={{0,8},{8,0},{1,9},{9,1},{2,10},{10,2},{3,11},{11,3},{4,12},{12,4},... | collective-permute-start | bytes 1769480 | tf_op jit(solution)/shard_map/ppermute | solution.py:32
  71.0 14.3 %all-to-all-start.2 = ((f32[16,4,1536]{2,1,0:T(4,128)}), f32[16,4,1536]{2,1,0:T(4,128)}, u32[]{:S(2)}, u32[]{:S(2)}) async-start(f32[16,4,1536]{2,1,0:T(4,128)} %add.81), calls=%async_computation.2 | async-start | bytes 786432 | tf_op jit(solution)/shard_map/all_to_all | solution.py:48
  79.6 0.9 copy-start.1
  80.5 1.2 copy-start.4
  85.3 24.3 %all-to-all-start.3 = ((bf16[16,96,512]{2,1,0:T(8,128)(2,1)}), bf16[16,96,512]{2,1,0:T(8,128)(2,1)S(1)}, u32[]{:S(2)}, u32[]{:S(2)}) async-start(bf16[16,96,512]{2,1,0:T(8,128)(2,1)} %copy-done.4), calls=%async_computation.3 | async-start | bytes 3145728 | tf_op jit(solution)/shard_map/all_to_all | solution.py:48
  90.1 3.4 %collective-permute-start.5 = (f32[4,1536]{1,0:T(4,128)S(1)}, f32[4,1536]{1,0:T(4,128)S(1)}, u32[]{:S(2)}, u32[]{:S(2)}) collective-permute-start(f32[4,1536]{1,0:T(4,128)S(1)} %reduce_sum.58), channel_id=1, source_target_pairs={{0,1},{1,0},{2,3},{3,2},{4,5},{5,4},{6,7},{7,6},{8,9},{9,8},{10,11... | collective-permute-start | bytes 73736 | tf_op jit(solution)/shard_map/ppermute | solution.py:37
  93.5 4.0 %collective-permute-start.6 = (f32[4,1536]{1,0:T(4,128)S(1)}, f32[4,1536]{1,0:T(4,128)S(1)}, u32[]{:S(2)}, u32[]{:S(2)}) collective-permute-start(f32[4,1536]{1,0:T(4,128)S(1)} %add.82), channel_id=1, source_target_pairs={{0,2},{1,3},{2,0},{3,1},{4,6},{5,7},{6,4},{7,5},{8,10},{9,11},{10,... | collective-permute-start | bytes 73736 | tf_op jit(solution)/shard_map/ppermute | solution.py:37
  97.4 6.7 %collective-permute-start.7 = (f32[4,1536]{1,0:T(4,128)S(1)}, f32[4,1536]{1,0:T(4,128)S(1)}, u32[]{:S(2)}, u32[]{:S(2)}) collective-permute-start(f32[4,1536]{1,0:T(4,128)S(1)} %add.83), channel_id=1, source_target_pairs={{0,4},{1,5},{2,6},{3,7},{4,0},{5,1},{6,2},{7,3},{8,12},{9,13},{10,... | collective-permute-start | bytes 73736 | tf_op jit(solution)/shard_map/ppermute | solution.py:37
  104.1 5.3 %collective-permute-start.8 = (f32[1,1536]{1,0:T(1,128)S(1)}, f32[1,1536]{1,0:T(1,128)S(1)}, u32[]{:S(2)}, u32[]{:S(2)}) collective-permute-start(f32[1,1536]{1,0:T(1,128)S(1)} %slice.80), channel_id=1, source_target_pairs={{0,8},{8,0},{1,9},{9,1},{2,10},{10,2},{3,11},{11,3},{4,12},{12,4},... | collective-permute-start | bytes 18440 | tf_op jit(solution)/shard_map/ppermute | solution.py:37
  109.6 1.2 copy-start.2
  110.8 0.9 copy-start.3
  111.7 20.8 %all-to-all-start.4 = ((bf16[16,112,256]{2,1,0:T(8,128)(2,1)}), bf16[16,112,256]{2,1,0:T(8,128)(2,1)}, u32[]{:S(2)}, u32[]{:S(2)}) async-start(bf16[16,112,256]{2,1,0:T(8,128)(2,1)} %copy-done.3), calls=%async_computation.4 | async-start | bytes 1835008 | tf_op jit(solution)/shard_map/all_to_all | solution.py:48
  118.6 4.5 %copy-start.6 = (f32[224,1536]{1,0:T(8,128)S(1)}, f32[224,1536]{1,0:T(8,128)}, u32[]{:S(2)}) copy-start(f32[224,1536]{1,0:T(8,128)} %copy-done.5) | copy-start | bytes 4128772
  134.7 8.5 %collective-permute-start.9 = (f32[16,1536]{1,0:T(8,128)S(1)}, f32[16,1536]{1,0:T(8,128)S(1)}, u32[]{:S(2)}, u32[]{:S(2)}) collective-permute-start(f32[16,1536]{1,0:T(8,128)S(1)} %get-tuple-element.68), channel_id=1, source_target_pairs={{0,8},{8,0},{1,9},{9,1},{2,10},{10,2},{3,11},{11,3},{4,12},{12,4},... | collective-permute-start | bytes 294920 | tf_op jit(solution)/shard_map/ppermute | solution.py:37
  138.1 13.3 %all-to-all-start.5 = ((bf16[16,6,768]{2,1,0:T(8,128)(2,1)}), bf16[16,6,768]{2,1,0:T(8,128)(2,1)S(1)}, u32[]{:S(2)}, u32[]{:S(2)}) async-start(bf16[16,6,768]{2,1,0:T(8,128)(2,1)} %get-tuple-element.69), calls=%async_computation.5 | async-start | bytes 393216 | tf_op jit(solution)/shard_map/all_to_all | solution.py:48
